TPU v7x, 512 devices: a whole 4x4x16 slice. The times are simulated.
512 devices in a mesh: blk: 512 (over z, y, x, core).
Axes of the slice: x: 4, y: 4, z: 16, core: 2. Of those that a mesh axis runs over, the one named last changes fastest.
Arguments:
- picture_vectors: float32 [131072, 1152], P('blk'), may hold values from -1.5909903 to 1.5909903
- caption_vectors: float32 [131072, 1152], P('blk'), may hold values from -2.2391715 to 2.2391715
- sharpness_factor: float32 [1], replicated, may hold values from 6 to 14
- additive_shift_term: float32 [1], replicated, may hold values from -7 to -4
Outputs:
- loss_rows: float32 [131072], P('blk')
- grad_image: float32 [131072, 1152], P('blk')
- text_gradient: float32 [131072, 1152], P('blk')
All inputs are finite; a program needn't handle non-finite values.
Results may differ from a plain program's by a relative error of at most 0.0003.
Values sent between devices are 32-bit elements; how exact they have to be, the bound alone decides.
No kernel may reach another device: no remote copies, remote signals or barrier semaphores. Data moves between devices by JAX's collectives and lax.ppermute only.
A program may use at most 64 MiB of HBM per device.

v0:
```python
import jax
import jax.numpy as jnp
from jax import lax
from jax.sharding import PartitionSpec as P

HOPS = 4


EPS = 1e-06
HIGH = lax.Precision.HIGHEST


def from_behind(value, axis, by):
    count = lax.axis_size(axis)
    return lax.ppermute(value, axis, [(i, (i + by) % count) for i in range(count)])


def normalize(raw):
    inverse_norm = lax.rsqrt(jnp.sum(raw * raw, axis=-1, keepdims=True) + EPS)
    return (raw * inverse_norm, inverse_norm)


def restore(raw, inverse_norm, grad):
    inner = jnp.sum(raw * grad, axis=-1, keepdims=True)
    return inverse_norm * grad - inverse_norm * inverse_norm * inverse_norm * inner * raw


def pair_tile(left, partner, similarity_multiplier, block_offset, positive):
    logits = jnp.dot(left, partner.T, precision=HIGH, preferred_element_type=jnp.float32)
    rolled_text = similarity_multiplier * logits + block_offset
    terms = jax.nn.softplus(rolled_text - 2.0 * positive * rolled_text)
    weight = similarity_multiplier * (jax.nn.sigmoid(rolled_text) - positive)
    return (terms, weight)


def transpose_product(weight, left):
    return lax.dot_general(
        weight, left, (((0,), (0,)), ((), ())), precision=HIGH, preferred_element_type=jnp.float32
    )


def body(picture_vectors, caption_vectors, sharpness_factor, additive_shift_term):
    rows = picture_vectors.shape[0]
    image_unit, inv_image = normalize(picture_vectors)
    caption_direction, inv_text = normalize(caption_vectors)
    similarity_multiplier = sharpness_factor[0]
    block_offset = additive_shift_term[0]
    loss = jnp.zeros((rows,), jnp.float32)
    grad_left = jnp.zeros_like(picture_vectors)
    visiting = caption_direction
    travel = jnp.zeros_like(caption_vectors)
    for step in range(HOPS):
        if step == 0:
            positive = jnp.eye(rows, dtype=jnp.float32)
        else:
            positive = jnp.zeros((rows, rows), jnp.float32)
        if step + 1 < HOPS:
            upcoming = from_behind(visiting, "blk", 1)
        terms, weight = pair_tile(
            image_unit, visiting, similarity_multiplier, block_offset, positive
        )
        loss = loss + jnp.sum(terms, axis=-1)
        grad_left = grad_left + jnp.dot(
            weight, visiting, precision=HIGH, preferred_element_type=jnp.float32
        )
        share = transpose_product(weight, image_unit)
        travel = travel + share
        if step + 1 < HOPS:
            travel = from_behind(travel, "blk", 1)
            visiting = upcoming
    text_grad = from_behind(travel, "blk", -(HOPS - 1))
    loss_rows = loss / HOPS
    grad_image = restore(picture_vectors, inv_image, grad_left)
    text_gradient = restore(caption_vectors, inv_text, text_grad)
    return (loss_rows, grad_image, text_gradient)


def solution(mesh):
    placed = (P("blk", None), P("blk", None), P(), P())
    return jax.shard_map(
        body,
        mesh=mesh,
        in_specs=placed,
        out_specs=(P("blk"), P("blk", None), P("blk", None)),
        check_vma=False,
    )
```

profile of v0, /device:TPU:1, one launch (start us, length us, event | category | flops | bytes accessed | tf_op | source)
XLA Modules:
  0.0 127.4 jit_solution(10941663050356976940)
XLA Ops:
  0.6 1.5 %multiply_reduce_fusion.2 = f32[256]{0:T(256)S(1)} fusion(f32[256,1152]{1,0:T(8,128)} %param.5), kind=kLoop, calls=%fused_computation.8 | loop fusion | flops 589568 | bytes 1180672 | tf_op jit(solution)/shard_map/reduce_sum | solution.py:19
  2.4 4.6 %collective-permute-start = (f32[256,1152]{1,0:T(8,128)S(1)}, f32[256,1152]{1,0:T(8,128)S(1)}, u32[]{:S(2)}, u32[]{:S(2)}) collective-permute-start(f32[256,1152]{1,0:T(8,128)S(1)} %broadcast_multiply_fusion), channel_id=1, source_target_pairs={{0,1},{1,2},{2,3},{3,4},{4,5},{5,6},{6,7},{7,8},{8,9},{9,10},{10,1... | collective-permute-start | bytes 3538952 | tf_op jit(solution)/shard_map/ppermute | solution.py:15
  8.5 1.5 %fusion.23 = (f32[256]{0:T(256)S(1)}, f32[256,256]{0,1:T(8,128)S(1)}) fusion(f32[]{:T(128)} %bitcast.22, f32[256,1152]{1,0:T(8,128)S(1)} %broadcast_multiply_fusion, f32[256,1152]{1,0:T(8,128)S(1)} %copy-done, f32[256]{0:T(256)S(1)} %add_rsqrt_fusion.1, f32[]{:T(128)} %bitcast.10), kind=kOutput, calls=%fused_computation.46 | convolution fusion | flops 907116288 | bytes 2623496 | tf_op jit(solution)/shard_map/dot_general | solution.py:29
  10.1 1.4 %fusion.9 = f32[256,1152]{1,0:T(8,128)S(1)} fusion(f32[256,1152]{1,0:T(8,128)S(1)} %copy-done, f32[256]{0:T(256)S(1)} %add_rsqrt_fusion.1, f32[256,256]{0,1:T(8,128)S(1)} %get-tuple-element.8, f32[]{:T(128)} %bitcast.21), kind=kOutput, calls=%fused_computation.27 | convolution fusion | flops 906723328 | bytes 2622468 | tf_op jit(solution)/shard_map/dot_general | solution.py:37
  11.5 1.9 %collective-permute-start.3 = (f32[256,1152]{1,0:T(8,128)S(1)}, f32[256,1152]{1,0:T(8,128)S(1)}, u32[]{:S(2)}, u32[]{:S(2)}) collective-permute-start(f32[256,1152]{1,0:T(8,128)S(1)} %fusion.9), channel_id=1, source_target_pairs={{0,1},{1,2},{2,3},{3,4},{4,5},{5,6},{6,7},{7,8},{8,9},{9,10},{10,1... | collective-permute-start | bytes 3538952 | tf_op jit(solution)/shard_map/ppermute | solution.py:15
  13.4 6.8 %collective-permute-done = f32[256,1152]{1,0:T(8,128)S(1)} collective-permute-done((f32[256,1152]{1,0:T(8,128)S(1)}, f32[256,1152]{1,0:T(8,128)S(1)}, u32[]{:S(2)}, u32[]{:S(2)}) %collective-permute-start) | collective-permute-done | bytes 1179680 | tf_op jit(solution)/shard_map/ppermute | solution.py:15
  20.2 4.4 %collective-permute-start.1 = (f32[256,1152]{1,0:T(8,128)S(1)}, f32[256,1152]{1,0:T(8,128)S(1)}, u32[]{:S(2)}, u32[]{:S(2)}) collective-permute-start(f32[256,1152]{1,0:T(8,128)S(1)} %collective-permute-done), channel_id=1, source_target_pairs={{0,1},{1,2},{2,3},{3,4},{4,5},{5,6},{6,7},{7,8},{8,9},{9,10},{10,1... | collective-permute-start | bytes 3538952 | tf_op jit(solution)/shard_map/ppermute | solution.py:15
  24.6 1.5 %fusion.24 = (f32[256]{0:T(256)S(1)}, f32[256,256]{0,1:T(8,128)S(1)}) fusion(f32[]{:T(128)} %bitcast.25, f32[256,1152]{1,0:T(8,128)S(1)} %collective-permute-done, f32[256,1152]{1,0:T(8,128)S(1)} %copy-done, f32[256]{0:T(256)S(1)} %add_rsqrt_fusion.1, f32[]{:T(128)} %bitcast.17), kind=kOutput, calls=%fused_computation.47 | convolution fusion | flops 906985216 | bytes 2623496 | tf_op jit(solution)/shard_map/dot_general | solution.py:29
  26.1 6.7 %collective-permute-done.3 = f32[256,1152]{1,0:T(8,128)S(1)} collective-permute-done((f32[256,1152]{1,0:T(8,128)S(1)}, f32[256,1152]{1,0:T(8,128)S(1)}, u32[]{:S(2)}, u32[]{:S(2)}) %collective-permute-start.3) | collective-permute-done | bytes 1179680 | tf_op jit(solution)/shard_map/ppermute | solution.py:15
  32.8 1.4 %convolution_add_fusion = f32[256,1152]{1,0:T(8,128)S(1)} fusion(f32[256,1152]{1,0:T(8,128)S(1)} %collective-permute-done.3, f32[256,1152]{1,0:T(8,128)S(1)} %copy-done, f32[256]{0:T(256)S(1)} %add_rsqrt_fusion.1, f32[256,256]{0,1:T(8,128)S(1)} %get-tuple-element.10, f32[]{:T(128)} %bitcast.18), kind=kOutput, calls=%fused_computation | convolution fusion | flops 906821632 | bytes 3802116 | tf_op jit(solution)/shard_map/dot_general | solution.py:37
  34.2 4.4 %collective-permute-start.4 = (f32[256,1152]{1,0:T(8,128)S(1)}, f32[256,1152]{1,0:T(8,128)S(1)}, u32[]{:S(2)}, u32[]{:S(2)}) collective-permute-start(f32[256,1152]{1,0:T(8,128)S(1)} %convolution_add_fusion), channel_id=1, source_target_pairs={{0,1},{1,2},{2,3},{3,4},{4,5},{5,6},{6,7},{7,8},{8,9},{9,10},{10,1... | collective-permute-start | bytes 3538952 | tf_op jit(solution)/shard_map/ppermute | solution.py:15
  39.9 5.5 %collective-permute-done.1 = f32[256,1152]{1,0:T(8,128)S(1)} collective-permute-done((f32[256,1152]{1,0:T(8,128)S(1)}, f32[256,1152]{1,0:T(8,128)S(1)}, u32[]{:S(2)}, u32[]{:S(2)}) %collective-permute-start.1) | collective-permute-done | bytes 1179680 | tf_op jit(solution)/shard_map/ppermute | solution.py:15
  45.5 4.4 %collective-permute-start.2 = (f32[256,1152]{1,0:T(8,128)S(1)}, f32[256,1152]{1,0:T(8,128)S(1)}, u32[]{:S(2)}, u32[]{:S(2)}) collective-permute-start(f32[256,1152]{1,0:T(8,128)S(1)} %collective-permute-done.1), channel_id=1, source_target_pairs={{0,1},{1,2},{2,3},{3,4},{4,5},{5,6},{6,7},{7,8},{8,9},{9,10},{10,1... | collective-permute-start | bytes 3538952 | tf_op jit(solution)/shard_map/ppermute | solution.py:15
  49.8 1.5 %fusion.25 = (f32[256]{0:T(256)S(1)}, f32[256,256]{0,1:T(8,128)S(1)}) fusion(f32[]{:T(128)} %bitcast.24, f32[256,1152]{1,0:T(8,128)S(1)} %collective-permute-done.1, f32[256,1152]{1,0:T(8,128)S(1)} %copy-done, f32[256]{0:T(256)S(1)} %add_rsqrt_fusion.1, f32[]{:T(128)} %bitcast.16), kind=kOutput, calls=%fused_computation.48 | convolution fusion | flops 906985216 | bytes 2623496 | tf_op jit(solution)/shard_map/dot_general | solution.py:29
  51.4 1.4 %fusion.6 = f32[256,1152]{1,0:T(8,128)S(1)} fusion(f32[256,1152]{1,0:T(8,128)S(1)} %copy-done, f32[256]{0:T(256)S(1)} %add_rsqrt_fusion.1, f32[256,256]{0,1:T(8,128)S(1)} %get-tuple-element.6, f32[]{:T(128)} %bitcast.19), kind=kOutput, calls=%fused_computation.24 | convolution fusion | flops 906526720 | bytes 2622468 | tf_op jit(solution)/shard_map/dot_general | solution.py:37
  52.8 5.3 %collective-permute-done.4 = f32[256,1152]{1,0:T(8,128)S(1)} collective-permute-done((f32[256,1152]{1,0:T(8,128)S(1)}, f32[256,1152]{1,0:T(8,128)S(1)}, u32[]{:S(2)}, u32[]{:S(2)}) %collective-permute-start.4) | collective-permute-done | bytes 1179680 | tf_op jit(solution)/shard_map/ppermute | solution.py:15
  58.2 4.6 %collective-permute-start.5 = (f32[256,1152]{1,0:T(8,128)S(1)}, f32[256,1152]{1,0:T(8,128)S(1)}, u32[]{:S(2)}, u32[]{:S(2)}) collective-permute-start(f32[256,1152]{1,0:T(8,128)S(1)} %add.114), channel_id=1, source_target_pairs={{0,1},{1,2},{2,3},{3,4},{4,5},{5,6},{6,7},{7,8},{8,9},{9,10},{10,1... | collective-permute-start | bytes 3538952 | tf_op jit(solution)/shard_map/ppermute | solution.py:15
  65.4 5.3 %collective-permute-done.2 = f32[256,1152]{1,0:T(8,128)S(1)} collective-permute-done((f32[256,1152]{1,0:T(8,128)S(1)}, f32[256,1152]{1,0:T(8,128)S(1)}, u32[]{:S(2)}, u32[]{:S(2)}) %collective-permute-start.2) | collective-permute-done | bytes 1179680 | tf_op jit(solution)/shard_map/ppermute | solution.py:15
  70.7 1.5 %fusion.26 = (f32[256]{0:T(256)S(1)}, f32[256,256]{0,1:T(8,128)S(1)}) fusion(f32[]{:T(128)} %bitcast.23, f32[256,1152]{1,0:T(8,128)S(1)} %collective-permute-done.2, f32[256,1152]{1,0:T(8,128)S(1)} %copy-done, f32[256]{0:T(256)S(1)} %add_rsqrt_fusion.1, f32[]{:T(128)} %bitcast.15), kind=kOutput, calls=%fused_computation.49 | convolution fusion | flops 906985216 | bytes 2623496 | tf_op jit(solution)/shard_map/dot_general | solution.py:29
  72.3 1.4 %fusion.4 = f32[256,1152]{1,0:T(8,128)S(1)} fusion(f32[256,1152]{1,0:T(8,128)S(1)} %copy-done, f32[256]{0:T(256)S(1)} %add_rsqrt_fusion.1, f32[256,256]{0,1:T(8,128)S(1)} %get-tuple-element.4, f32[]{:T(128)} %bitcast.20), kind=kOutput, calls=%fused_computation.22 | convolution fusion | flops 906526720 | bytes 2622468 | tf_op jit(solution)/shard_map/dot_general | solution.py:37
  73.7 9.7 %collective-permute-done.5 = f32[256,1152]{1,0:T(8,128)S(1)} collective-permute-done((f32[256,1152]{1,0:T(8,128)S(1)}, f32[256,1152]{1,0:T(8,128)S(1)}, u32[]{:S(2)}, u32[]{:S(2)}) %collective-permute-start.5) | collective-permute-done | bytes 1179680 | tf_op jit(solution)/shard_map/ppermute | solution.py:15
  83.5 17.0 %collective-permute-start.6 = (f32[256,1152]{1,0:T(8,128)S(1)}, f32[256,1152]{1,0:T(8,128)S(1)}, u32[]{:S(2)}, u32[]{:S(2)}) collective-permute-start(f32[256,1152]{1,0:T(8,128)S(1)} %add.115), channel_id=1, source_target_pairs={{0,509},{1,510},{2,511},{3,0},{4,1},{5,2},{6,3},{7,4},{8,5},{9,6},... | collective-permute-start | bytes 3538952 | tf_op jit(solution)/shard_map/ppermute | solution.py:15
  100.5 1.5 %multiply_reduce_fusion.1 = (f32[256]{0:T(256)S(1)}, f32[256,1152]{1,0:T(8,128)S(1)}) fusion(f32[256,1152]{1,0:T(8,128)S(1)} %copy-done, f32[256,1152]{1,0:T(8,128)S(1)} %convolution_add_fusion.2, f32[256,1152]{1,0:T(8,128)S(1)} %collective-permute-done.2, f32[256,256]{0,1:T(8,128)S(1)} %get-tuple-element.4, f32[]{:T(128)} %bitcast.11), kind=kOutput, calls=%fused_computation.7 | convolution fusion | flops 907116288 | bytes 4981764 | tf_op jit(solution)/shard_map/dot_general | solution.py:63
  103.8 22.2 %collective-permute-done.6 = f32[256,1152]{1,0:T(8,128)S(1)} collective-permute-done((f32[256,1152]{1,0:T(8,128)S(1)}, f32[256,1152]{1,0:T(8,128)S(1)}, u32[]{:S(2)}, u32[]{:S(2)}) %collective-permute-start.6) | collective-permute-done | bytes 1179680 | tf_op jit(solution)/shard_map/ppermute | solution.py:15
  (19 shorter events, 7.7 us)
Async XLA Ops:
  0.6 1.6 %copy-start.1 = (f32[256,1152]{1,0:T(8,128)S(1)}, f32[256,1152]{1,0:T(8,128)}, u32[]{:S(2)}) copy-start(f32[256,1152]{1,0:T(8,128)} %param.5) | copy-start | bytes 3538948
  2.3 6.1 %copy-start = (f32[256,1152]{1,0:T(8,128)S(1)}, f32[256,1152]{1,0:T(8,128)}, u32[]{:S(2)}) copy-start(f32[256,1152]{1,0:T(8,128)} %param.4) | copy-start | bytes 3538948
  2.4 17.8 %collective-permute-start = (f32[256,1152]{1,0:T(8,128)S(1)}, f32[256,1152]{1,0:T(8,128)S(1)}, u32[]{:S(2)}, u32[]{:S(2)}) collective-permute-start(f32[256,1152]{1,0:T(8,128)S(1)} %broadcast_multiply_fusion), channel_id=1, source_target_pairs={{0,1},{1,2},{2,3},{3,4},{4,5},{5,6},{6,7},{7,8},{8,9},{9,10},{10,1... | collective-permute-start | bytes 3538952 | tf_op jit(solution)/shard_map/ppermute | solution.py:15
  11.5 21.3 %collective-permute-start.3 = (f32[256,1152]{1,0:T(8,128)S(1)}, f32[256,1152]{1,0:T(8,128)S(1)}, u32[]{:S(2)}, u32[]{:S(2)}) collective-permute-start(f32[256,1152]{1,0:T(8,128)S(1)} %fusion.9), channel_id=1, source_target_pairs={{0,1},{1,2},{2,3},{3,4},{4,5},{5,6},{6,7},{7,8},{8,9},{9,10},{10,1... | collective-permute-start | bytes 3538952 | tf_op jit(solution)/shard_map/ppermute | solution.py:15
  20.2 25.3 %collective-permute-start.1 = (f32[256,1152]{1,0:T(8,128)S(1)}, f32[256,1152]{1,0:T(8,128)S(1)}, u32[]{:S(2)}, u32[]{:S(2)}) collective-permute-start(f32[256,1152]{1,0:T(8,128)S(1)} %collective-permute-done), channel_id=1, source_target_pairs={{0,1},{1,2},{2,3},{3,4},{4,5},{5,6},{6,7},{7,8},{8,9},{9,10},{10,1... | collective-permute-start | bytes 3538952 | tf_op jit(solution)/shard_map/ppermute | solution.py:15
  34.2 23.9 %collective-permute-start.4 = (f32[256,1152]{1,0:T(8,128)S(1)}, f32[256,1152]{1,0:T(8,128)S(1)}, u32[]{:S(2)}, u32[]{:S(2)}) collective-permute-start(f32[256,1152]{1,0:T(8,128)S(1)} %convolution_add_fusion), channel_id=1, source_target_pairs={{0,1},{1,2},{2,3},{3,4},{4,5},{5,6},{6,7},{7,8},{8,9},{9,10},{10,1... | collective-permute-start | bytes 3538952 | tf_op jit(solution)/shard_map/ppermute | solution.py:15
  45.5 25.3 %collective-permute-start.2 = (f32[256,1152]{1,0:T(8,128)S(1)}, f32[256,1152]{1,0:T(8,128)S(1)}, u32[]{:S(2)}, u32[]{:S(2)}) collective-permute-start(f32[256,1152]{1,0:T(8,128)S(1)} %collective-permute-done.1), channel_id=1, source_target_pairs={{0,1},{1,2},{2,3},{3,4},{4,5},{5,6},{6,7},{7,8},{8,9},{9,10},{10,1... | collective-permute-start | bytes 3538952 | tf_op jit(solution)/shard_map/ppermute | solution.py:15
  58.2 25.2 %collective-permute-start.5 = (f32[256,1152]{1,0:T(8,128)S(1)}, f32[256,1152]{1,0:T(8,128)S(1)}, u32[]{:S(2)}, u32[]{:S(2)}) collective-permute-start(f32[256,1152]{1,0:T(8,128)S(1)} %add.114), channel_id=1, source_target_pairs={{0,1},{1,2},{2,3},{3,4},{4,5},{5,6},{6,7},{7,8},{8,9},{9,10},{10,1... | collective-permute-start | bytes 3538952 | tf_op jit(solution)/shard_map/ppermute | solution.py:15
  83.5 42.5 %collective-permute-start.6 = (f32[256,1152]{1,0:T(8,128)S(1)}, f32[256,1152]{1,0:T(8,128)S(1)}, u32[]{:S(2)}, u32[]{:S(2)}) collective-permute-start(f32[256,1152]{1,0:T(8,128)S(1)} %add.115), channel_id=1, source_target_pairs={{0,509},{1,510},{2,511},{3,0},{4,1},{5,2},{6,3},{7,4},{8,5},{9,6},... | collective-permute-start | bytes 3538952 | tf_op jit(solution)/shard_map/ppermute | solution.py:15
where the time goes:
time: 128 us; the launch traced here: 127 us
  waiting for transfers between devices  61.6 us (48%)
  starting transfers between devices  41.3 us (32%)
  matrix products  17 us (13%)
  other arithmetic  5.3 us (4%)
  between operations  2.07 us (2%)
    ppermute x7, waiting for transfers between devices, from_behind(): lax.ppermute(value, axis, [(i, (i + by) % count) for i in range(count)])  61.6 us
    ppermute x7, starting transfers between devices, from_behind(): lax.ppermute(value, axis, [(i, (i + by) % count) for i in range(count)])  41.3 us
    dot_general x4, matrix products, pair_tile(): jnp.dot(left, partner.T, precision=HIGH, preferred_element_type=jnp.float32)  6.06 us
    dot_general x4, matrix products, transpose_product(): lax.dot_general(weight, left, (((0,), (0,)), ((), ())), precision=HIGH, p...  5.6 us
    dot_general x4, matrix products, body(): jnp.dot(weight, visiting, precision=HIGH, preferred_element_type=jnp.floa...  5.35 us
  transfers between devices with their start and end apart: 7, of which 7 were waited for; matrix products, arithmetic and copies ran while one was open for 15% of the time, Pallas kernels for 0%

commit v1 on v0

v1 whole, which is shorter than its diff:
```python
import jax
import jax.numpy as jnp
from jax import lax
from jax.sharding import PartitionSpec as P

HOPS = 4
EPS = 1e-06
HIGH = lax.Precision.HIGH


def across(value):
    count = lax.axis_size("blk")
    pairs = [(i, (i + 1 if i % 2 else i - 1) % count) for i in range(count)]
    return lax.ppermute(value, "blk", pairs)


def in_chip(value):
    count = lax.axis_size("blk")
    return lax.ppermute(value, "blk", [(i, i ^ 1) for i in range(count)])


def normalize(raw):
    inverse_norm = lax.rsqrt(jnp.sum(raw * raw, axis=-1, keepdims=True) + EPS)
    return (raw * inverse_norm, inverse_norm)


def restore(raw, inverse_norm, grad):
    inner = jnp.sum(raw * grad, axis=-1, keepdims=True)
    return inverse_norm * grad - inverse_norm * inverse_norm * inverse_norm * inner * raw


def dot(a, b, ca, cb):
    return lax.dot_general(
        a, b, (((ca,), (cb,)), ((), ())), precision=HIGH, preferred_element_type=jnp.float32
    )


def body(picture_vectors, caption_vectors, sharpness_factor, additive_shift_term):
    rows = picture_vectors.shape[0]
    scale = sharpness_factor[0]
    shift = additive_shift_term[0]
    even = lax.axis_index("blk") % 2 == 0

    def pair(a, b, positive=None):
        shifted = scale * dot(a, b, 1, 1) + shift
        if positive is None:
            return jax.nn.softplus(shifted), scale * jax.nn.sigmoid(shifted)
        terms = jax.nn.softplus(shifted - 2.0 * positive * shifted)
        return terms, scale * (jax.nn.sigmoid(shifted) - positive)

    p_raw = jnp.where(even, picture_vectors, caption_vectors)
    q_raw = jnp.where(even, caption_vectors, picture_vectors)
    p, inv_p = normalize(p_raw)
    q, inv_q = normalize(q_raw)
    y1 = across(p)
    z = in_chip(q)
    y2 = across(z)
    terms, weight = pair(p, q, jnp.eye(rows, dtype=jnp.float32))
    loss_p = jnp.sum(terms, axis=1)
    loss_q = jnp.sum(terms, axis=0)
    grad_p = dot(weight, q, 1, 0)
    grad_q = dot(weight, p, 0, 0)
    terms, weight = pair(z, q)
    loss_q = loss_q + jnp.sum(terms, axis=0)
    grad_q = grad_q + dot(weight, z, 0, 0)
    y1s = in_chip(y1)
    terms, weight = pair(y1s, y1)
    back = dot(weight, y1s, 0, 0)
    back_loss = jnp.pad(jnp.sum(terms, axis=0)[None, :], ((0, 7), (0, back.shape[1] - rows)))
    returned = across(jnp.concatenate([back, back_loss], axis=0))
    terms, weight = pair(p, y1)
    loss_p = loss_p + jnp.sum(terms, axis=1)
    grad_p = grad_p + dot(weight, y1, 1, 0)
    terms, weight = pair(y1s, q)
    loss_q = loss_q + jnp.sum(terms, axis=0)
    grad_q = grad_q + dot(weight, y1s, 0, 0)
    y2s = in_chip(y2)
    terms, weight = pair(p, y2)
    loss_p = loss_p + jnp.sum(terms, axis=1)
    grad_p = grad_p + dot(weight, y2, 1, 0)
    terms, weight = pair(y2s, q)
    loss_q = loss_q + jnp.sum(terms, axis=0)
    grad_q = grad_q + dot(weight, y2s, 0, 0)
    out_q = restore(q_raw, inv_q, grad_q)
    grad_p = grad_p + returned[:rows]
    loss_p = loss_p + returned[rows, :rows]
    out_p = restore(p_raw, inv_p, grad_p)
    loss_rows = jnp.where(even, loss_p, loss_q) / HOPS
    grad_image = jnp.where(even, out_p, out_q)
    text_gradient = jnp.where(even, out_q, out_p)
    return (loss_rows, grad_image, text_gradient)


def solution(mesh):
    placed = (P("blk", None), P("blk", None), P(), P())
    return jax.shard_map(
        body,
        mesh=mesh,
        in_specs=placed,
        out_specs=(P("blk"), P("blk", None), P("blk", None)),
        check_vma=False,
    )
```

time: 128 us -> 84.2 us (0.66)
  waiting for transfers between devices: 61.6 us -> 24 us
  matrix products: 17 us -> 13.2 us
  starting transfers between devices: 41.3 us -> 39.8 us
    ppermute x7 -> x6, waiting for transfers between devices: 61.6 us -> 24 us  [the longest x3 24 us: across(): return lax.ppermute(value, 'blk', pairs)]
    dot_general x12 -> x15, matrix products: 17 us -> 13.2 us  [dot(): lax.dot_general(a, b, (((ca,), (cb,)), ((), ())), precision=HIGH, preferr...]
    sub x2 -> x0, other arithmetic: 2.43 us -> none  [restore(): inverse_norm * grad]
    select_n x0 -> x1, other arithmetic: none -> 1.82 us  [body(): text_gradient = jnp.where(even, out_q, out_p)]
    ppermute x7 -> x6, starting transfers between devices: 41.3 us -> 39.8 us  [the longest x3 31.3 us: in_chip(): return lax.ppermute(value, 'blk', [(i, i ^ 1) for i in range(count)])]
  transfers between devices with their start and end apart: 7 -> 6, of which waited for: 7 -> 2; matrix products, arithmetic and copies ran while one was open for 15% -> 15% of each run, Pallas kernels for 0% -> 0%
where the time goes in v1:
time: 84.2 us; the launch traced here: 83.9 us
  starting transfers between devices  39.8 us (47%)
  waiting for transfers between devices  24 us (29%)
  matrix products  13.2 us (16%)
  other arithmetic  4.75 us (6%)
  between operations  2.11 us (3%)
    ppermute x3, starting transfers between devices, in_chip(): return lax.ppermute(value, 'blk', [(i, i ^ 1) for i in range(count)])  31.3 us
    ppermute x3, waiting for transfers between devices, across(): return lax.ppermute(value, 'blk', pairs)  24 us
    dot_general x15, matrix products, dot(): lax.dot_general(a, b, (((ca,), (cb,)), ((), ())), precision=HIGH, preferr...  13.2 us
    ppermute x3, starting transfers between devices, across(): return lax.ppermute(value, 'blk', pairs)  8.53 us
    reduce_sum x1, other arithmetic, normalize(): inverse_norm = lax.rsqrt(jnp.sum(raw * raw, axis=-1, keepdims=True) + EPS)  1.96 us
    select_n x1, other arithmetic, body(): text_gradient = jnp.where(even, out_q, out_p)  1.82 us
  transfers between devices with their start and end apart: 6, of which 2 were waited for; matrix products, arithmetic and copies ran while one was open for 15% of the time, Pallas kernels for 0%

profile of v1, /device:TPU:1, one launch (start us, length us, event | category | flops | bytes accessed | tf_op | source)
XLA Modules:
  0.0 83.9 jit_solution(7644570825834431245)
XLA Ops:
  0.6 2.0 %multiply_reduce_fusion.3 = (f32[256]{0:T(256)S(1)}, f32[256,1152]{1,0:T(8,128)S(1)}, f32[256]{0:T(256)S(1)}, f32[256,1152]{1,0:T(8,128)S(1)}) fusion(f32[256,1152]{1,0:T(8,128)} %param.4, f32[256,1152]{1,0:T(8,128)} %param.5, pred[]{:T(512)S(6)} %eq.10), kind=kLoop, calls=%fused_computation.13 | loop fusion | flops 1768960 | bytes 4720641 | tf_op jit(solution)/shard_map/reduce_sum | solution.py:23
  2.8 4.5 %collective-permute-start = (f32[256,1152]{1,0:T(8,128)S(1)}, f32[256,1152]{1,0:T(8,128)S(1)}, u32[]{:S(2)}, u32[]{:S(2)}) collective-permute-start(f32[256,1152]{1,0:T(8,128)S(1)} %broadcast_multiply_fusion.1), channel_id=1, source_target_pairs={{0,511},{1,2},{2,1},{3,4},{4,3},{5,6},{6,5},{7,8},{8,7},{9,10},{10... | collective-permute-start | bytes 3538952 | tf_op jit(solution)/shard_map/ppermute | solution.py:14
  7.4 14.4 %collective-permute-start.1 = (f32[256,1152]{1,0:T(8,128)S(1)}, f32[256,1152]{1,0:T(8,128)S(1)}, u32[]{:S(2)}, u32[]{:S(2)}) collective-permute-start(f32[256,1152]{1,0:T(8,128)S(1)} %broadcast_multiply_fusion), channel_id=1, source_target_pairs={{0,1},{1,0},{2,3},{3,2},{4,5},{5,4},{6,7},{7,6},{8,9},{9,8},{10,11... | collective-permute-start | bytes 3538952 | tf_op jit(solution)/shard_map/ppermute | solution.py:19
  23.1 1.0 %fusion.58 = (f32[256]{0:T(256)S(1)}, f32[256]{0:T(256)S(1)}, f32[256,256]{1,0:T(8,128)S(1)}) fusion(f32[]{:T(128)} %bitcast.41, f32[256,1152]{1,0:T(8,128)S(1)} %broadcast_multiply_fusion.1, f32[256,1152]{1,0:T(8,128)S(1)} %broadcast_multiply_fusion, f32[]{:T(128)} %bitcast.26), kind=kOutput, calls=%fused_computation.94 | convolution fusion | flops 453901824 | bytes 2623496 | tf_op jit(solution)/shard_map/dot_general | solution.py:33
  24.1 0.8 fusion.59
  24.9 0.7 fusion.60
  25.7 9.8 %collective-permute-start.3 = (f32[256,1152]{1,0:T(8,128)S(1)}, f32[256,1152]{1,0:T(8,128)S(1)}, u32[]{:S(2)}, u32[]{:S(2)}) collective-permute-start(f32[256,1152]{1,0:T(8,128)S(1)} %collective-permute-done), channel_id=1, source_target_pairs={{0,1},{1,0},{2,3},{3,2},{4,5},{5,4},{6,7},{7,6},{8,9},{9,8},{10,11... | collective-permute-start | bytes 3538952 | tf_op jit(solution)/shard_map/ppermute | solution.py:19
  35.6 1.9 %collective-permute-start.2 = (f32[256,1152]{1,0:T(8,128)S(1)}, f32[256,1152]{1,0:T(8,128)S(1)}, u32[]{:S(2)}, u32[]{:S(2)}) collective-permute-start(f32[256,1152]{1,0:T(8,128)S(1)} %collective-permute-done.1), channel_id=1, source_target_pairs={{0,511},{1,2},{2,1},{3,4},{4,3},{5,6},{6,5},{7,8},{8,7},{9,10},{10... | collective-permute-start | bytes 3538952 | tf_op jit(solution)/shard_map/ppermute | solution.py:14
  37.5 0.9 %fusion.11 = (f32[256]{0:T(256)S(1)}, f32[256,256]{1,0:T(8,128)S(1)}) fusion(f32[]{:T(128)} %bitcast.44, f32[256,1152]{1,0:T(8,128)S(1)} %collective-permute-done.1, f32[256,1152]{1,0:T(8,128)S(1)} %broadcast_multiply_fusion, f32[]{:T(128)} %bitcast.35), kind=kOutput, calls=%fused_computation.45 | convolution fusion | flops 453574400 | bytes 2622472 | tf_op jit(solution)/shard_map/dot_general | solution.py:33
  38.4 1.0 %fusion.8 = (f32[256]{0:T(256)S(1)}, f32[256,256]{1,0:T(8,128)S(1)}) fusion(f32[]{:T(128)} %bitcast.47, f32[256,1152]{1,0:T(8,128)S(1)} %broadcast_multiply_fusion.1, f32[256,1152]{1,0:T(8,128)S(1)} %collective-permute-done, f32[]{:T(128)} %bitcast.39), kind=kOutput, calls=%fused_computation.42 | convolution fusion | flops 453574400 | bytes 2622472 | tf_op jit(solution)/shard_map/dot_general | solution.py:33
  39.4 0.8 convolution_add_fusion.2
  40.9 12.5 %collective-permute-done.2 = f32[256,1152]{1,0:T(8,128)S(1)} collective-permute-done((f32[256,1152]{1,0:T(8,128)S(1)}, f32[256,1152]{1,0:T(8,128)S(1)}, u32[]{:S(2)}, u32[]{:S(2)}) %collective-permute-start.2) | collective-permute-done | bytes 1179680 | tf_op jit(solution)/shard_map/ppermute | solution.py:14
  53.4 7.0 %collective-permute-start.5 = (f32[256,1152]{1,0:T(8,128)S(1)}, f32[256,1152]{1,0:T(8,128)S(1)}, u32[]{:S(2)}, u32[]{:S(2)}) collective-permute-start(f32[256,1152]{1,0:T(8,128)S(1)} %collective-permute-done.2), channel_id=1, source_target_pairs={{0,1},{1,0},{2,3},{3,2},{4,5},{5,4},{6,7},{7,6},{8,9},{9,8},{10,11... | collective-permute-start | bytes 3538952 | tf_op jit(solution)/shard_map/ppermute | solution.py:19
  60.4 0.9 %fusion.10 = (f32[256]{0:T(256)S(1)}, f32[256,256]{1,0:T(8,128)S(1)}) fusion(f32[]{:T(128)} %bitcast.45, f32[256,1152]{1,0:T(8,128)S(1)} %collective-permute-done.3, f32[256,1152]{1,0:T(8,128)S(1)} %collective-permute-done, f32[]{:T(128)} %bitcast.37), kind=kOutput, calls=%fused_computation.44 | convolution fusion | flops 453574400 | bytes 2622472 | tf_op jit(solution)/shard_map/dot_general | solution.py:33
  61.3 0.8 fusion.39
  62.2 2.1 %collective-permute-start.4 = (f32[264,1152]{1,0:T(8,128)S(1)}, f32[264,1152]{1,0:T(8,128)S(1)}, u32[]{:S(2)}, u32[]{:S(2)}) collective-permute-start(f32[264,1152]{1,0:T(8,128)S(1)} %select_maximum_fusion), channel_id=1, source_target_pairs={{0,511},{1,2},{2,1},{3,4},{4,3},{5,6},{6,5},{7,8},{8,7},{9,10},{10... | collective-permute-start | bytes 3649544 | tf_op jit(solution)/shard_map/ppermute | solution.py:14
  64.3 0.9 %fusion.12 = (f32[256]{0:T(256)S(1)}, f32[256,256]{1,0:T(8,128)S(1)}) fusion(f32[]{:T(128)} %bitcast.43, f32[256,1152]{1,0:T(8,128)S(1)} %collective-permute-done.3, f32[256,1152]{1,0:T(8,128)S(1)} %broadcast_multiply_fusion, f32[]{:T(128)} %bitcast.34), kind=kOutput, calls=%fused_computation.46 | convolution fusion | flops 453574400 | bytes 2622472 | tf_op jit(solution)/shard_map/dot_general | solution.py:33
  65.2 1.0 %fusion.9 = (f32[256]{0:T(256)S(1)}, f32[256,256]{1,0:T(8,128)S(1)}) fusion(f32[]{:T(128)} %bitcast.46, f32[256,1152]{1,0:T(8,128)S(1)} %broadcast_multiply_fusion.1, f32[256,1152]{1,0:T(8,128)S(1)} %collective-permute-done.2, f32[]{:T(128)} %bitcast.38), kind=kOutput, calls=%fused_computation.43 | convolution fusion | flops 453574400 | bytes 2622472 | tf_op jit(solution)/shard_map/dot_general | solution.py:33
  66.2 0.8 convolution_add_fusion.1
  67.0 0.9 %fusion.13 = (f32[256]{0:T(256)S(1)}, f32[256,256]{1,0:T(8,128)S(1)}) fusion(f32[]{:T(128)} %bitcast.42, f32[256,1152]{1,0:T(8,128)S(1)} %collective-permute-done.5, f32[256,1152]{1,0:T(8,128)S(1)} %broadcast_multiply_fusion, f32[]{:T(128)} %bitcast.33), kind=kOutput, calls=%fused_computation.47 | convolution fusion | flops 453574400 | bytes 2622472 | tf_op jit(solution)/shard_map/dot_general | solution.py:33
  67.9 1.0 %multiply_reduce_fusion = (f32[256]{0:T(256)S(1)}, f32[256,1152]{1,0:T(8,128)S(1)}) fusion(f32[256,1152]{1,0:T(8,128)S(1)} %get-tuple-element.12, f32[256,1152]{1,0:T(8,128)S(1)} %convolution_add_fusion.1, f32[256,1152]{1,0:T(8,128)S(1)} %collective-permute-done.5, f32[256,256]{1,0:T(8,128)S(1)} %get-tuple-element.14, f32[]{:T(128)} %bitcast.27), kind=kOutput, calls=%fused_computation.9 | convolution fusion | flops 454131456 | bytes 4981764 | tf_op jit(solution)/shard_map/dot_general | solution.py:33
  68.9 11.5 %collective-permute-done.4 = f32[264,1152]{1,0:T(8,128)S(1)} collective-permute-done((f32[264,1152]{1,0:T(8,128)S(1)}, f32[264,1152]{1,0:T(8,128)S(1)}, u32[]{:S(2)}, u32[]{:S(2)}) %collective-permute-start.4) | collective-permute-done | bytes 1216544 | tf_op jit(solution)/shard_map/ppermute | solution.py:14
  80.4 1.0 %multiply_reduce_fusion.1 = (f32[256]{0:T(256)S(1)}, f32[256,1152]{1,0:T(8,128)S(1)}) fusion(f32[256,1152]{1,0:T(8,128)S(1)} %get-tuple-element.6, f32[264,1152]{1,0:T(8,128)S(1)} %collective-permute-done.4, f32[256,1152]{1,0:T(8,128)S(1)} %convolution_add_fusion.4, f32[256,1152]{1,0:T(8,128)S(1)} %collective-permute-done.2, ...), kind=kOutput, calls=%fused_computation.11 | convolution fusion | flops 454426368 | bytes 6161412 | tf_op jit(solution)/shard_map/dot_general | solution.py:33
  81.5 1.8 %broadcast_select_fusion = (f32[256,1152]{1,0:T(8,128)}, f32[256,1152]{1,0:T(8,128)}) fusion(pred[]{:T(512)S(6)} %eq.10, f32[256,1152]{1,0:T(8,128)S(1)} %get-tuple-element.6, f32[256]{0:T(256)S(1)} %fusion.61, f32[256,1152]{1,0:T(8,128)S(1)} %get-tuple-element.27, f32[256]{0:T(256)S(1)} %add_rsqrt_fusion.1, f32[256,1152]{1,0:T(8,128)S(1)} %get-tuple-element.12, ...), kind=kLoop, calls=%fused_computation.37 | loop fusion | flops 2359296 | bytes 7081985 | tf_op jit(solution)/shard_map/jit(_where)/select_n | solution.py:90
  (14 shorter events, 1.7 us)
Async XLA Ops:
  2.8 22.9 %collective-permute-start = (f32[256,1152]{1,0:T(8,128)S(1)}, f32[256,1152]{1,0:T(8,128)S(1)}, u32[]{:S(2)}, u32[]{:S(2)}) collective-permute-start(f32[256,1152]{1,0:T(8,128)S(1)} %broadcast_multiply_fusion.1), channel_id=1, source_target_pairs={{0,511},{1,2},{2,1},{3,4},{4,3},{5,6},{6,5},{7,8},{8,7},{9,10},{10... | collective-permute-start | bytes 3538952 | tf_op jit(solution)/shard_map/ppermute | solution.py:14
  7.4 28.1 %collective-permute-start.1 = (f32[256,1152]{1,0:T(8,128)S(1)}, f32[256,1152]{1,0:T(8,128)S(1)}, u32[]{:S(2)}, u32[]{:S(2)}) collective-permute-start(f32[256,1152]{1,0:T(8,128)S(1)} %broadcast_multiply_fusion), channel_id=1, source_target_pairs={{0,1},{1,0},{2,3},{3,2},{4,5},{5,4},{6,7},{7,6},{8,9},{9,8},{10,11... | collective-permute-start | bytes 3538952 | tf_op jit(solution)/shard_map/ppermute | solution.py:19
  25.7 34.7 %collective-permute-start.3 = (f32[256,1152]{1,0:T(8,128)S(1)}, f32[256,1152]{1,0:T(8,128)S(1)}, u32[]{:S(2)}, u32[]{:S(2)}) collective-permute-start(f32[256,1152]{1,0:T(8,128)S(1)} %collective-permute-done), channel_id=1, source_target_pairs={{0,1},{1,0},{2,3},{3,2},{4,5},{5,4},{6,7},{7,6},{8,9},{9,8},{10,11... | collective-permute-start | bytes 3538952 | tf_op jit(solution)/shard_map/ppermute | solution.py:19
  35.6 17.8 %collective-permute-start.2 = (f32[256,1152]{1,0:T(8,128)S(1)}, f32[256,1152]{1,0:T(8,128)S(1)}, u32[]{:S(2)}, u32[]{:S(2)}) collective-permute-start(f32[256,1152]{1,0:T(8,128)S(1)} %collective-permute-done.1), channel_id=1, source_target_pairs={{0,511},{1,2},{2,1},{3,4},{4,3},{5,6},{6,5},{7,8},{8,7},{9,10},{10... | collective-permute-start | bytes 3538952 | tf_op jit(solution)/shard_map/ppermute | solution.py:14
  53.4 13.6 %collective-permute-start.5 = (f32[256,1152]{1,0:T(8,128)S(1)}, f32[256,1152]{1,0:T(8,128)S(1)}, u32[]{:S(2)}, u32[]{:S(2)}) collective-permute-start(f32[256,1152]{1,0:T(8,128)S(1)} %collective-permute-done.2), channel_id=1, source_target_pairs={{0,1},{1,0},{2,3},{3,2},{4,5},{5,4},{6,7},{7,6},{8,9},{9,8},{10,11... | collective-permute-start | bytes 3538952 | tf_op jit(solution)/shard_map/ppermute | solution.py:19
  62.2 18.2 %collective-permute-start.4 = (f32[264,1152]{1,0:T(8,128)S(1)}, f32[264,1152]{1,0:T(8,128)S(1)}, u32[]{:S(2)}, u32[]{:S(2)}) collective-permute-start(f32[264,1152]{1,0:T(8,128)S(1)} %select_maximum_fusion), channel_id=1, source_target_pairs={{0,511},{1,2},{2,1},{3,4},{4,3},{5,6},{6,5},{7,8},{8,7},{9,10},{10... | collective-permute-start | bytes 3649544 | tf_op jit(solution)/shard_map/ppermute | solution.py:14

commit v2 on v1

--- a/solution.py
+++ b/solution.py
@@ -14,9 +14,11 @@
     return lax.ppermute(value, "blk", pairs)
 
 
-def in_chip(value):
+def in_chip(value, even):
     count = lax.axis_size("blk")
-    return lax.ppermute(value, "blk", [(i, i ^ 1) for i in range(count)])
+    groups = [[i, i + 1] for i in range(0, count, 2)]
+    both = lax.all_gather(value, "blk", axis_index_groups=groups)
+    return jnp.where(even, both[1], both[0])
 
 
 def normalize(raw):
@@ -53,8 +55,15 @@
     p, inv_p = normalize(p_raw)
     q, inv_q = normalize(q_raw)
     y1 = across(p)
-    z = in_chip(q)
+    z = in_chip(q, even)
     y2 = across(z)
+    y1s = in_chip(y1, even)
+    terms, weight = pair(y1s, y1)
+    back = dot(weight, y1s, 0, 0)
+    back_loss = jnp.pad(jnp.sum(terms, axis=0)[None, :], ((0, 7), (0, back.shape[1] - rows)))
+    sent = (jnp.concatenate([back, back_loss], axis=0))
+    returned = across(sent)
+    p, q, z, y1, y1s, sent = lax.optimization_barrier((p, q, z, y1, y1s, sent))
     terms, weight = pair(p, q, jnp.eye(rows, dtype=jnp.float32))
     loss_p = jnp.sum(terms, axis=1)
     loss_q = jnp.sum(terms, axis=0)
@@ -63,18 +72,13 @@
     terms, weight = pair(z, q)
     loss_q = loss_q + jnp.sum(terms, axis=0)
     grad_q = grad_q + dot(weight, z, 0, 0)
-    y1s = in_chip(y1)
-    terms, weight = pair(y1s, y1)
-    back = dot(weight, y1s, 0, 0)
-    back_loss = jnp.pad(jnp.sum(terms, axis=0)[None, :], ((0, 7), (0, back.shape[1] - rows)))
-    returned = across(jnp.concatenate([back, back_loss], axis=0))
     terms, weight = pair(p, y1)
     loss_p = loss_p + jnp.sum(terms, axis=1)
     grad_p = grad_p + dot(weight, y1, 1, 0)
     terms, weight = pair(y1s, q)
     loss_q = loss_q + jnp.sum(terms, axis=0)
     grad_q = grad_q + dot(weight, y1s, 0, 0)
-    y2s = in_chip(y2)
+    y2s = in_chip(y2, even)
     terms, weight = pair(p, y2)
     loss_p = loss_p + jnp.sum(terms, axis=1)
     grad_p = grad_p + dot(weight, y2, 1, 0)

time: 84.2 us -> 119 us (1.41)
  starting transfers between devices: 39.8 us -> 9.31 us
  waiting for transfers between devices: 24 us -> 48 us
  matrix products: 13.2 us -> 30.8 us
  between operations: 2.11 us -> 15.3 us
  other arithmetic: 4.75 us -> 11.8 us
  local copies, waits for them, and re-layouts: 0.01 us -> 3.44 us
    all_gather x0 -> x3, waiting for transfers between devices: none -> 33.8 us  [in_chip(): both = lax.all_gather(value, 'blk', axis_index_groups=groups)]
    ppermute x3 -> x0, starting transfers between devices: 31.3 us -> none  [in_chip(): return lax.ppermute(value, 'blk', [(i, i ^ 1) for i in range(count)])]
    dot_general x15, matrix products: 13.2 us -> 30.8 us  [dot(): lax.dot_general(a, b, (((ca,), (cb,)), ((), ())), precision=HIGH, preferr...]
    ppermute x3, waiting for transfers between devices: 24 us -> 14.2 us  [across(): return lax.ppermute(value, 'blk', pairs)]
    select_n x0 -> x2, other arithmetic: none -> 4.51 us  [in_chip(): return jnp.where(even, both[1], both[0])]
    unnamed x0 -> x42, local copies, waits for them, and re-layouts: none -> 2.17 us
    slice x1, local copies, waits for them, and re-layouts: 0.01 us -> 1.27 us  [body(): loss_p = loss_p + returned[rows, :rows]]
  transfers between devices with their start and end apart: 6 -> 6, of which waited for: 2 -> 4; matrix products, arithmetic and copies ran while one was open for 15% -> 27% of each run, Pallas kernels for 0% -> 0%
where the time goes in v2:
time: 119 us
  waiting for transfers between devices  48 us (40%)
  matrix products  30.8 us (26%)
  between operations  15.3 us (13%)
  other arithmetic  11.8 us (10%)
  starting transfers between devices  9.31 us (8%)
  local copies, waits for them, and re-layouts  3.44 us (3%)
    all_gather x3, waiting for transfers between devices, in_chip(): both = lax.all_gather(value, 'blk', axis_index_groups=groups)  33.8 us
    dot_general x15, matrix products, dot(): lax.dot_general(a, b, (((ca,), (cb,)), ((), ())), precision=HIGH, preferr...  30.8 us
    ppermute x3, waiting for transfers between devices, across(): return lax.ppermute(value, 'blk', pairs)  14.2 us
    ppermute x3, starting transfers between devices, across(): return lax.ppermute(value, 'blk', pairs)  9.19 us
    select_n x2, other arithmetic, in_chip(): return jnp.where(even, both[1], both[0])  4.51 us
  transfers between devices with their start and end apart: 6, of which 4 were waited for; matrix products, arithmetic and copies ran while one was open for 27% of the time, Pallas kernels for 0%

profile of v2, /device:TPU:1, one launch (start us, length us, event | category | flops | bytes accessed | tf_op | source)
XLA Modules:
  0.0 118.8 jit_solution(12422291533707002562)
XLA Ops:
  7.2 2.0 %multiply_reduce_fusion.2 = (f32[256]{0:T(256)S(1)}, f32[256,1152]{1,0:T(8,128)S(1)}, f32[256]{0:T(256)S(1)}, f32[256,1152]{1,0:T(8,128)S(1)}) fusion(f32[256,1152]{1,0:T(8,128)} %param.5, f32[256,1152]{1,0:T(8,128)} %param.4, pred[]{:T(512)S(6)} %eq.10), kind=kLoop, calls=%fused_computation.15 | loop fusion | flops 1768960 | bytes 4720641 | tf_op jit(solution)/shard_map/reduce_sum | solution.py:25
  11.6 4.5 %collective-permute-start = (f32[256,1152]{1,0:T(8,128)S(1)}, f32[256,1152]{1,0:T(8,128)S(1)}, u32[]{:S(2)}, u32[]{:S(2)}) collective-permute-start(f32[256,1152]{1,0:T(8,128)S(1)} %broadcast_multiply_fusion.1), channel_id=1, source_target_pairs={{0,511},{1,2},{2,1},{3,4},{4,3},{5,6},{6,5},{7,8},{8,7},{9,10},{10... | collective-permute-start | bytes 3538952 | tf_op jit(solution)/shard_map/ppermute | solution.py:14
  16.2 14.2 %collective-permute-done = f32[256,1152]{1,0:T(8,128)S(1)} collective-permute-done((f32[256,1152]{1,0:T(8,128)S(1)}, f32[256,1152]{1,0:T(8,128)S(1)}, u32[]{:S(2)}, u32[]{:S(2)}) %collective-permute-start) | collective-permute-done | bytes 1179680 | tf_op jit(solution)/shard_map/ppermute | solution.py:14
  32.7 7.0 %all-gather.7.cloned.1.call-done = f32[512,1152]{1,0:T(8,128)} async-done(((f32[256,1152]{1,0:T(8,128)}), f32[512,1152]{1,0:T(8,128)}) %all-gather.7.cloned.1.call-update) | async-done | bytes 2359312 | tf_op jit(solution)/shard_map/all_gather | solution.py:20
  39.8 2.8 %slice_select_fusion.2 = f32[256,1152]{1,0:T(8,128)} fusion(f32[512,1152]{1,0:T(8,128)} %all-gather.7.cloned.1.call-done, pred[]{:T(512)S(6)} %eq.10), kind=kLoop, calls=%fused_computation.10 | loop fusion | flops 294912 | bytes 3538945 | tf_op jit(solution)/shard_map/jit(_where)/select_n | solution.py:21
  42.5 2.3 %collective-permute-start.1 = (f32[256,1152]{1,0:T(8,128)}, f32[256,1152]{1,0:T(8,128)}, u32[]{:S(2)}, u32[]{:S(2)}) collective-permute-start(f32[256,1152]{1,0:T(8,128)} %slice_select_fusion.2), channel_id=1, source_target_pairs={{0,511},{1,2},{2,1},{3,4},{4,3},{5,6},{6,5},{7,8},{8,7},{9,10},{10... | collective-permute-start | bytes 3538952 | tf_op jit(solution)/shard_map/ppermute | solution.py:14
  44.8 19.8 %all-gather.9.cloned.1.call-done = f32[512,1152]{1,0:T(8,128)} async-done(((f32[256,1152]{1,0:T(8,128)}), f32[512,1152]{1,0:T(8,128)}) %all-gather.9.cloned.1.call-update) | async-done | bytes 2359312 | tf_op jit(solution)/shard_map/all_gather | solution.py:20
  64.6 1.7 %slice_select_fusion.1 = f32[256,1152]{1,0:T(8,128)S(1)} fusion(f32[512,1152]{1,0:T(8,128)} %all-gather.9.cloned.1.call-done, pred[]{:T(512)S(6)} %eq.10), kind=kLoop, calls=%fused_computation.9 | loop fusion | flops 294912 | bytes 3538945 | tf_op jit(solution)/shard_map/jit(_where)/select_n | solution.py:21
  69.2 2.4 %collective-permute-start.2 = (f32[264,1152]{1,0:T(8,128)}, f32[264,1152]{1,0:T(8,128)}, u32[]{:S(2)}, u32[]{:S(2)}) collective-permute-start(f32[264,1152]{1,0:T(8,128)} %select_maximum_fusion), channel_id=1, source_target_pairs={{0,511},{1,2},{2,1},{3,4},{4,3},{5,6},{6,5},{7,8},{8,7},{9,10},{10... | collective-permute-start | bytes 3649544 | tf_op jit(solution)/shard_map/ppermute | solution.py:14
  71.6 2.8 %fusion.15 = (f32[256]{0:T(256)}, f32[256,256]{1,0:T(8,128)S(1)}) fusion(f32[]{:T(128)} %bitcast.42, f32[256,1152]{1,0:T(8,128)} %slice_select_fusion.2, f32[256,1152]{1,0:T(8,128)S(1)} %copy-done, f32[]{:T(128)} %bitcast.33), kind=kOutput, calls=%fused_computation.49 | convolution fusion | flops 453574400 | bytes 2622472 | tf_op jit(solution)/shard_map/dot_general | solution.py:35
  74.3 3.1 %fusion.29 = f32[256,1152]{1,0:T(8,128)} fusion(f32[256,1152]{1,0:T(8,128)} %slice_select_fusion.2, f32[256,256]{1,0:T(8,128)S(1)} %get-tuple-element.31, f32[]{:T(128)} %bitcast.27), kind=kOutput, calls=%fused_computation.63 | convolution fusion | flops 453246976 | bytes 2621444 | tf_op jit(solution)/shard_map/dot_general | solution.py:35
  77.5 2.1 %fusion.16 = (f32[256]{0:T(256)}, f32[256,256]{1,0:T(8,128)}) fusion(f32[]{:T(128)} %bitcast.41, f32[256,1152]{1,0:T(8,128)S(1)} %slice_select_fusion.1, f32[256,1152]{1,0:T(8,128)S(1)} %copy-done, f32[]{:T(128)} %bitcast.32), kind=kOutput, calls=%fused_computation.50 | convolution fusion | flops 453574400 | bytes 2622472 | tf_op jit(solution)/shard_map/dot_general | solution.py:35
  79.6 2.7 %fusion.23 = f32[256,1152]{1,0:T(8,128)} fusion(f32[256,1152]{1,0:T(8,128)S(1)} %slice_select_fusion.1, f32[256,256]{1,0:T(8,128)} %get-tuple-element.28, f32[]{:T(128)} %bitcast.26), kind=kOutput, calls=%fused_computation.57 | convolution fusion | flops 453246976 | bytes 2621444 | tf_op jit(solution)/shard_map/dot_general | solution.py:35
  82.4 1.6 %fusion.66 = (f32[256]{0:T(256)}, f32[256]{0:T(256)}, f32[256,256]{1,0:T(8,128)S(1)}) fusion(f32[]{:T(128)} %bitcast.45, f32[256,1152]{1,0:T(8,128)S(1)} %broadcast_multiply_fusion.1, f32[256,1152]{1,0:T(8,128)S(1)} %copy-done, f32[]{:T(128)} %bitcast.36), kind=kOutput, calls=%fused_computation.102 | convolution fusion | flops 453901824 | bytes 2623496 | tf_op jit(solution)/shard_map/dot_general | solution.py:35
  84.0 1.6 %fusion.13 = (f32[256]{0:T(256)}, f32[256,256]{1,0:T(8,128)S(1)}) fusion(f32[]{:T(128)} %bitcast.44, f32[256,1152]{1,0:T(8,128)S(1)} %broadcast_multiply_fusion.1, f32[256,1152]{1,0:T(8,128)S(1)} %copy-done.3, f32[]{:T(128)} %bitcast.35), kind=kOutput, calls=%fused_computation.47 | convolution fusion | flops 453574400 | bytes 2622472 | tf_op jit(solution)/shard_map/dot_general | solution.py:35
  86.3 2.8 %fusion.14 = (f32[256]{0:T(256)}, f32[256,256]{1,0:T(8,128)S(1)}) fusion(f32[]{:T(128)} %bitcast.43, f32[256,1152]{1,0:T(8,128)S(1)} %broadcast_multiply_fusion.1, f32[256,1152]{1,0:T(8,128)} %collective-permute-done.1, f32[]{:T(128)} %bitcast.34), kind=kOutput, calls=%fused_computation.48 | convolution fusion | flops 453574400 | bytes 2622472 | tf_op jit(solution)/shard_map/dot_general | solution.py:35
  89.0 2.1 %fusion.35 = f32[256,1152]{1,0:T(8,128)S(1)} fusion(f32[256,1152]{1,0:T(8,128)} %collective-permute-done.1, f32[256,256]{1,0:T(8,128)S(1)} %get-tuple-element.33, f32[]{:T(128)} %bitcast.28), kind=kOutput, calls=%fused_computation.69 | convolution fusion | flops 453246976 | bytes 2621444 | tf_op jit(solution)/shard_map/dot_general | solution.py:35
  91.1 1.3 %slice.42 = f32[1,256]{1,0:T(1,128)} slice(f32[264,1152]{1,0:T(8,128)} %collective-permute-done.2), slice={[256:257], [0:256]} | slice | bytes 2048 | tf_op jit(solution)/shard_map/slice | solution.py:90
  92.4 3.3 %multiply_reduce_fusion.1 = (f32[256]{0:T(256)S(1)}, f32[256,1152]{1,0:T(8,128)}) fusion(f32[256,1152]{1,0:T(8,128)S(1)} %copy-done.7, f32[264,1152]{1,0:T(8,128)} %collective-permute-done.2, f32[256,1152]{1,0:T(8,128)S(1)} %fusion.35, f32[256,1152]{1,0:T(8,128)S(1)} %fusion.41, f32[256,1152]{1,0:T(8,128)S(1)} %copy-done, ...), kind=kOutput, calls=%fused_computation.14 | convolution fusion | flops 454917888 | bytes 7341060 | tf_op jit(solution)/shard_map/dot_general | solution.py:35
  96.3 6.9 %all-gather.11.cloned.1.call-done = f32[512,1152]{1,0:T(8,128)} async-done(((f32[256,1152]{1,0:T(8,128)}), f32[512,1152]{1,0:T(8,128)}) %all-gather.11.cloned.1.call-update) | async-done | bytes 2359312 | tf_op jit(solution)/shard_map/all_gather | solution.py:20
  103.2 2.6 %fusion.17 = (f32[256]{0:T(256)S(1)}, f32[256,256]{1,0:T(8,128)S(1)}) fusion(f32[]{:T(128)} %bitcast.40, f32[256,1152]{1,0:T(8,128)S(1)} %copy-done, f32[512,1152]{1,0:T(8,128)} %all-gather.11.cloned.1.call-done, pred[]{:T(512)S(6)} %eq.10, f32[]{:T(128)} %bitcast.31), kind=kOutput, calls=%fused_computation.51 | convolution fusion | flops 453869312 | bytes 3802121 | tf_op jit(solution)/shard_map/dot_general | solution.py:35
  105.9 2.5 %fusion.11 = f32[256,1152]{1,0:T(8,128)S(1)} fusion(f32[512,1152]{1,0:T(8,128)} %all-gather.11.cloned.1.call-done, pred[]{:T(512)S(6)} %eq.10, f32[256,256]{1,0:T(8,128)S(1)} %get-tuple-element.26, f32[]{:T(128)} %bitcast.25), kind=kOutput, calls=%fused_computation.45 | convolution fusion | flops 453541888 | bytes 3801093 | tf_op jit(solution)/shard_map/dot_general | solution.py:35
  108.5 1.2 %multiply_reduce_fusion = (f32[256]{0:T(256)S(1)}, f32[256,1152]{1,0:T(8,128)S(1)}) fusion(f32[256,1152]{1,0:T(8,128)S(1)} %copy-done.5, f32[256,1152]{1,0:T(8,128)S(1)} %fusion.11, f32[256,1152]{1,0:T(8,128)S(1)} %copy-done.10, f32[256,1152]{1,0:T(8,128)S(1)} %copy-done.9, f32[256,1152]{1,0:T(8,128)S(1)} %broadcast_multiply_fusion.1, ...), kind=kOutput, calls=%fused_computation.12 | convolution fusion | flops 454917888 | bytes 7341060 | tf_op jit(solution)/shard_map/dot_general | solution.py:35
  109.8 1.8 %broadcast_select_fusion = (f32[256,1152]{1,0:T(8,128)}, f32[256,1152]{1,0:T(8,128)}) fusion(pred[]{:T(512)S(6)} %eq.10, f32[256,1152]{1,0:T(8,128)S(1)} %copy-done.7, f32[256]{0:T(256)S(1)} %copy-done.19, f32[256,1152]{1,0:T(8,128)S(1)} %copy-done.8, f32[256]{0:T(256)S(1)} %add_rsqrt_fusion.1, f32[256,1152]{1,0:T(8,128)S(1)} %copy-done.5, ...), kind=kLoop, calls=%fused_computation.40 | loop fusion | flops 2359296 | bytes 7081985 | tf_op jit(solution)/shard_map/jit(_where)/select_n | solution.py:94
  (61 shorter events, 8.3 us)
Async XLA Ops:
  7.2 32.6 %all-gather.7.cloned.1.call-start = ((), (), s32[]{:S(2)}) async-start(), calls=%async_computation | async-start | bytes 3538944 | tf_op jit(solution)/shard_map/all_gather | solution.py:20
  9.2 2.3 %copy-start.6 = (f32[256,1152]{1,0:T(8,128)}, f32[256,1152]{1,0:T(8,128)S(1)}, u32[]{:S(2)}) copy-start(f32[256,1152]{1,0:T(8,128)S(1)} %get-tuple-element.22) | copy-start | bytes 3538948
  11.4 53.2 %all-gather.9.cloned.1.call-start = ((), (), s32[]{:S(2)}) async-start(), calls=%async_computation.1 | async-start | bytes 3538944 | tf_op jit(solution)/shard_map/all_gather | solution.py:20
  11.6 18.7 %collective-permute-start = (f32[256,1152]{1,0:T(8,128)S(1)}, f32[256,1152]{1,0:T(8,128)S(1)}, u32[]{:S(2)}, u32[]{:S(2)}) collective-permute-start(f32[256,1152]{1,0:T(8,128)S(1)} %broadcast_multiply_fusion.1), channel_id=1, source_target_pairs={{0,511},{1,2},{2,1},{3,4},{4,3},{5,6},{6,5},{7,8},{8,7},{9,10},{10... | collective-permute-start | bytes 3538952 | tf_op jit(solution)/shard_map/ppermute | solution.py:14
  31.4 71.8 %all-gather.11.cloned.1.call-start = ((), (), s32[]{:S(2)}) async-start(), calls=%async_computation.2 | async-start | bytes 3538944 | tf_op jit(solution)/shard_map/all_gather | solution.py:20
  42.5 23.9 %copy-start.2 = (f32[256,1152]{1,0:T(8,128)S(1)}, f32[256,1152]{1,0:T(8,128)}, u32[]{:S(2)}) copy-start(f32[256,1152]{1,0:T(8,128)} %copy-done.1) | copy-start | bytes 3538948
  42.5 37.1 %collective-permute-start.1 = (f32[256,1152]{1,0:T(8,128)}, f32[256,1152]{1,0:T(8,128)}, u32[]{:S(2)}, u32[]{:S(2)}) collective-permute-start(f32[256,1152]{1,0:T(8,128)} %slice_select_fusion.2), channel_id=1, source_target_pairs={{0,511},{1,2},{2,1},{3,4},{4,3},{5,6},{6,5},{7,8},{8,7},{9,10},{10... | collective-permute-start | bytes 3538952 | tf_op jit(solution)/shard_map/ppermute | solution.py:14
  68.1 3.5 %copy-start = (f32[256,1152]{1,0:T(8,128)S(1)}, f32[256,1152]{1,0:T(8,128)}, u32[]{:S(2)}) copy-start(f32[256,1152]{1,0:T(8,128)} %broadcast_multiply_fusion) | copy-start | bytes 3538948
  69.2 21.9 %collective-permute-start.2 = (f32[264,1152]{1,0:T(8,128)}, f32[264,1152]{1,0:T(8,128)}, u32[]{:S(2)}, u32[]{:S(2)}) collective-permute-start(f32[264,1152]{1,0:T(8,128)} %select_maximum_fusion), channel_id=1, source_target_pairs={{0,511},{1,2},{2,1},{3,4},{4,3},{5,6},{6,5},{7,8},{8,7},{9,10},{10... | collective-permute-start | bytes 3649544 | tf_op jit(solution)/shard_map/ppermute | solution.py:14
  82.4 1.6 %copy-start.3 = (f32[256,1152]{1,0:T(8,128)S(1)}, f32[256,1152]{1,0:T(8,128)}, u32[]{:S(2)}) copy-start(f32[256,1152]{1,0:T(8,128)} %copy-done.1) | copy-start | bytes 3538948
  84.0 8.5 %copy-start.11 = (f32[256,256]{1,0:T(8,128)}, f32[256,256]{1,0:T(8,128)S(1)}, u32[]{:S(2)}) copy-start(f32[256,256]{1,0:T(8,128)S(1)} %get-tuple-element.29) | copy-start | bytes 786436
  89.0 3.4 %copy-start.7 = (f32[256,1152]{1,0:T(8,128)S(1)}, f32[256,1152]{1,0:T(8,128)}, u32[]{:S(2)}) copy-start(f32[256,1152]{1,0:T(8,128)} %copy-done.6) | copy-start | bytes 3538948
  103.2 5.2 %copy-start.10 = (f32[256,1152]{1,0:T(8,128)S(1)}, f32[256,1152]{1,0:T(8,128)}, u32[]{:S(2)}) copy-start(f32[256,1152]{1,0:T(8,128)} %fusion.23) | copy-start | bytes 3538948
  105.8 2.6 %copy-start.5 = (f32[256,1152]{1,0:T(8,128)S(1)}, f32[256,1152]{1,0:T(8,128)}, u32[]{:S(2)}) copy-start(f32[256,1152]{1,0:T(8,128)} %copy-done.4) | copy-start | bytes 3538948
  105.9 2.6 %copy-start.9 = (f32[256,1152]{1,0:T(8,128)S(1)}, f32[256,1152]{1,0:T(8,128)}, u32[]{:S(2)}) copy-start(f32[256,1152]{1,0:T(8,128)} %fusion.29) | copy-start | bytes 3538948
  105.9 2.6 %copy-start.12 = (f32[256,256]{1,0:T(8,128)S(1)}, f32[256,256]{1,0:T(8,128)}, u32[]{:S(2)}) copy-start(f32[256,256]{1,0:T(8,128)} %copy-done.11) | copy-start | bytes 786436
  108.5 1.3 %copy-start.8 = (f32[256,1152]{1,0:T(8,128)S(1)}, f32[256,1152]{1,0:T(8,128)}, u32[]{:S(2)}) copy-start(f32[256,1152]{1,0:T(8,128)} %get-tuple-element.37) | copy-start | bytes 3538948
  109.7 1.9 %copy-start.13 = (f32[256]{0:T(256)S(1)}, f32[256]{0:T(256)}, u32[]{:S(2)}) copy-start(f32[256]{0:T(256)} %get-tuple-element.30) | copy-start | bytes 3076
  109.7 1.9 %copy-start.14 = (f32[256]{0:T(256)S(1)}, f32[256]{0:T(256)}, u32[]{:S(2)}) copy-start(f32[256]{0:T(256)} %get-tuple-element.27) | copy-start | bytes 3076
  109.7 1.9 %copy-start.15 = (f32[256]{0:T(256)S(1)}, f32[256]{0:T(256)}, u32[]{:S(2)}) copy-start(f32[256]{0:T(256)} %get-tuple-element.13) | copy-start | bytes 3076
  109.8 1.9 %copy-start.16 = (f32[256]{0:T(256)S(1)}, f32[256]{0:T(256)}, u32[]{:S(2)}) copy-start(f32[256]{0:T(256)} %get-tuple-element.14) | copy-start | bytes 3076
  109.8 1.9 %copy-start.17 = (f32[256]{0:T(256)S(1)}, f32[256]{0:T(256)}, u32[]{:S(2)}) copy-start(f32[256]{0:T(256)} %get-tuple-element.34) | copy-start | bytes 3076
  109.8 1.9 %copy-start.18 = (f32[256]{0:T(256)S(1)}, f32[256]{0:T(256)}, u32[]{:S(2)}) copy-start(f32[256]{0:T(256)} %get-tuple-element.32) | copy-start | bytes 3076
  109.8 1.9 %copy-start.20 = (f32[1,256]{1,0:T(1,128)S(1)}, f32[1,256]{1,0:T(1,128)}, u32[]{:S(2)}) copy-start(f32[1,256]{1,0:T(1,128)} %slice.42) | copy-start | bytes 3076
  (3 other events, 3.3 us)
Sparse Core Ops, SparseCore 0:
  11.5 28.1 all-gather.6
  41.8 22.7 all-gather.8
  79.8 23.3 all-gather.10

commit v3 on v1

v3 whole, which is shorter than its diff:
```python
import functools

import jax
import jax.numpy as jnp
from jax import lax
from jax.experimental import pallas as pl
from jax.experimental.pallas import tpu as pltpu
from jax.sharding import PartitionSpec as P

HOPS = 4
EPS = 1e-06
F32 = jnp.float32
BF16 = jnp.bfloat16
CHUNKS = 4
PAD = 8
VMEM_LIMIT = 24 * 1024 * 1024


def across(value):
    count = lax.axis_size("blk")
    pairs = [(i, (i + 1 if i % 2 else i - 1) % count) for i in range(count)]
    return lax.ppermute(value, "blk", pairs)


def in_chip(value):
    count = lax.axis_size("blk")
    return lax.ppermute(value, "blk", [(i, i ^ 1) for i in range(count)])


def split(value):
    high = value.astype(BF16)
    return high, (value - high.astype(F32)).astype(BF16)


def product(a, b, contract):
    def one(x, y):
        return lax.dot_general(x, y, (contract, ((), ())), preferred_element_type=F32)

    return one(a[0], b[0]) + (one(a[0], b[1]) + one(a[1], b[0]))


def logits(rows, others):
    return product(rows, others, ((1,), (1,)))


def pair_terms(logit, scale, shift, own=False):
    shifted = scale * logit + shift
    decay = jnp.exp(-jnp.abs(shifted))
    part = 1.0 / (1.0 + decay)
    sigmoid = jnp.where(shifted >= 0.0, part, decay * part)
    signed = shifted
    if own:
        shape = shifted.shape
        positive = lax.broadcasted_iota(jnp.int32, shape, 0) == lax.broadcasted_iota(jnp.int32, shape, 1)
        signed = jnp.where(positive, -shifted, shifted)
        sigmoid = sigmoid - jnp.where(positive, 1.0, 0.0)
    return jnp.maximum(signed, 0.0) + jnp.log1p(decay), scale * sigmoid


def spread(weight, others):
    return product(split(weight), others, ((1,), (0,)))


def step(number):
    return pl.when(lax.axis_index("blk") < (1 << 20) + number)


def row_sums(terms):
    sums = jnp.sum(terms, axis=1, keepdims=True)
    return jnp.transpose(jnp.broadcast_to(sums, (terms.shape[0], 128)))[:8]


def pick_kernel(odd_takes, image, text, unit, inverse, raw, sem):
    rows = raw.shape[0] // CHUNKS
    takes_image = lax.rem(lax.axis_index("blk"), 2) != odd_takes

    def copy(source, c):
        part = pl.ds(c * rows, rows)
        return pltpu.make_async_copy(source.at[part], raw.at[part], sem.at[c])

    @pl.when(takes_image)
    def _():
        for c in range(CHUNKS):
            copy(image, c).start()

    @pl.when(jnp.logical_not(takes_image))
    def _():
        for c in range(CHUNKS):
            copy(text, c).start()

    extra = unit.shape[0] - raw.shape[0]
    if extra:
        unit[raw.shape[0] :] = jnp.zeros((extra, raw.shape[1]), F32)
    for c in range(CHUNKS):
        copy(image, c).wait()
        part = pl.ds(c * rows, rows)
        value = raw[part]
        inv = lax.rsqrt(jnp.sum(value * value, axis=1, keepdims=True) + EPS)
        unit[part] = value * inv
        inverse[part] = jnp.broadcast_to(inv, (rows, 128))


def middle_kernel(scale, shift, y1, y1s, sent, tile, hi, lo):
    rows, width = y1s.shape

    @step(0)
    def _():
        hi[...], lo[...] = split(y1s[...])
        tile[...] = logits(split(y1[:rows]), (hi[...], lo[...]))

    @step(1)
    def _():
        terms, weight = pair_terms(tile[...], scale[0], shift[0])
        sent[:rows] = spread(weight, (hi[...], lo[...]))
        sent[rows:, :rows] = row_sums(terms)
        sent[rows:, rows:] = jnp.zeros((8, width - rows), F32)


def local_kernel(
    scale, shift, p_ref, q, z, y1, y1s, after, grad_p, grad_q, loss_p, loss_q, ph, plo, qh, qlo,
    zh, zl, yh, yl, sh, sl, tile_own, tile_z, tile_y, tile_s
):
    rows = q.shape[0]

    @step(0)
    def _():
        ph[...], plo[...] = split(p_ref[:rows])
        qh[...], qlo[...] = split(q[...])
        tile_own[...] = logits((ph[...], plo[...]), (qh[...], qlo[...]))
        zh[...], zl[...] = split(z[...])
        tile_z[...] = logits((qh[...], qlo[...]), (zh[...], zl[...]))
        yh[...], yl[...] = split(y1[:rows])
        tile_y[...] = logits((ph[...], plo[...]), (yh[...], yl[...]))
        sh[...], sl[...] = split(y1s[...])
        tile_s[...] = logits((qh[...], qlo[...]), (sh[...], sl[...]))

    @step(1)
    def _():
        terms_own, weight_own = pair_terms(tile_own[...], scale[0], shift[0], own=True)
        terms_y, weight_y = pair_terms(tile_y[...], scale[0], shift[0])
        loss_p[...] = terms_own + terms_y
        tile_own[...] = jnp.transpose(weight_own)
        grad_p[...] = spread(weight_own, (qh[...], qlo[...])) + spread(weight_y, (yh[...], yl[...]))
        loss_q[...] = jnp.transpose(terms_own)

    @step(2)
    def _():
        terms_z, weight_z = pair_terms(tile_z[...], scale[0], shift[0])
        terms_s, weight_s = pair_terms(tile_s[...], scale[0], shift[0])
        loss_q[...] += terms_z + terms_s
        grad_q[...] = (
            spread(tile_own[...], (ph[...], plo[...]))
            + spread(weight_z, (zh[...], zl[...]))
            + spread(weight_s, (sh[...], sl[...]))
        )


def restored(unit, inverse, grad):
    inner = jnp.sum(unit * grad, axis=1, keepdims=True)
    return inverse * (grad - inner * unit)


def put(value_ref, image_out, text_out, to_image, sem, c, rows):
    part = pl.ds(c * rows, rows)

    @pl.when(to_image)
    def _():
        pltpu.make_async_copy(value_ref.at[part], image_out.at[part], sem.at[c]).start()

    @pl.when(jnp.logical_not(to_image))
    def _():
        pltpu.make_async_copy(value_ref.at[part], text_out.at[part], sem.at[c]).start()


def finish(unit, inverse, grad, image_out, text_out, result, sem, to_image):
    rows = result.shape[0] // CHUNKS
    for c in range(CHUNKS):
        part = pl.ds(c * rows, rows)
        result[part] = restored(unit[part], inverse[part][:, :1], grad(part))
        put(result, image_out, text_out, to_image, sem, c, rows)
    for c in range(CHUNKS):
        part = pl.ds(c * rows, rows)
        pltpu.make_async_copy(result.at[part], image_out.at[part], sem.at[c]).wait()


def second_kernel(
    scale, shift, ph, plo, qh, qlo, y2, y2s, gp_in, gq_in, lp_in, lq_in, q, inv_q,
    image_out, text_out, grad_p, loss_p, loss_q, grad_q, yh, yl, sh, sl, tile_y, tile_s, result, sem
):
    rows = q.shape[0]

    @step(0)
    def _():
        yh[...], yl[...] = split(y2[:rows])
        tile_y[...] = logits((ph[...], plo[...]), (yh[...], yl[...]))
        sh[...], sl[...] = split(y2s[...])
        tile_s[...] = logits((qh[...], qlo[...]), (sh[...], sl[...]))

    @step(1)
    def _():
        terms_s, weight_s = pair_terms(tile_s[...], scale[0], shift[0])
        grad_q[...] = gq_in[...] + spread(weight_s, (sh[...], sl[...]))
        terms_y, weight_y = pair_terms(tile_y[...], scale[0], shift[0])
        grad_p[...] = gp_in[...] + spread(weight_y, (yh[...], yl[...]))
        loss_p[...] = row_sums(lp_in[...] + terms_y)
        loss_q[...] = row_sums(lq_in[...] + terms_s)

    odd = lax.rem(lax.axis_index("blk"), 2) == 1
    finish(q, inv_q, lambda part: grad_q[part], image_out, text_out, result, sem, odd)


def last_kernel(
    gp_in, returned, p, inv_p, loss_p, loss_q, image_in, text_in, loss, image_out, text_out, result, sem
):
    rows = result.shape[0]
    even = lax.rem(lax.axis_index("blk"), 2) == 0
    total = jnp.where(even, loss_p[:1] + returned[rows : rows + 1, :rows], loss_q[:1])
    loss[...] = total * (1.0 / HOPS)
    finish(
        p, inv_p, lambda part: gp_in[part] + returned[part], image_out, text_out, result, sem, even
    )


def call(kernel, ins, outs, scratch=(), aliases=None):
    arrays, specs = [], []
    for array, place in ins:
        specs.append(pl.BlockSpec(memory_space=place))
        arrays.append(pltpu.with_memory_space_constraint(array, place) if place in (pltpu.VMEM, pltpu.HBM) else array)
    return pl.pallas_call(
        kernel,
        out_shape=[o for o, _ in outs],
        in_specs=specs,
        out_specs=[pl.BlockSpec(memory_space=place) for _, place in outs],
        scratch_shapes=list(scratch),
        input_output_aliases=aliases or {},
        compiler_params=pltpu.CompilerParams(vmem_limit_bytes=VMEM_LIMIT),
        cost_estimate=pl.CostEstimate(flops=0, transcendentals=0, bytes_accessed=0),
    )(*arrays)


def body(picture_vectors, caption_vectors, sharpness_factor, additive_shift_term):
    rows, width = picture_vectors.shape
    block = (rows, width)
    vm, hbm, sm, anywhere = pltpu.VMEM, pltpu.HBM, pltpu.SMEM, pl.ANY

    def fast(shape=block, dtype=F32):
        return (pltpu.VMEM(shape, dtype), vm)

    scalars = [(sharpness_factor, sm), (additive_shift_term, sm)]

    def v(*arrays):
        return [(a, vm) for a in arrays]

    def pick(odd_takes, taken):
        return call(
            functools.partial(pick_kernel, odd_takes),
            [(picture_vectors, hbm), (caption_vectors, hbm)],
            [fast((taken, width)), fast((rows, 128))],
            [pltpu.VMEM(block, F32), pltpu.SemaphoreType.DMA((CHUNKS,))],
        )

    line, square, half = (8, rows), (rows, rows), pltpu.VMEM(block, BF16)
    p, inv_p = pick(1, rows + PAD)
    y1 = across(p)
    q, inv_q = pick(0, rows)
    z = in_chip(q)
    y2 = across(jnp.pad(z, ((0, PAD), (0, 0))))
    y1s = in_chip(y1[:rows])
    (sent,) = call(
        middle_kernel,
        scalars + v(y1, y1s),
        [fast((rows + 8, width))],
        [pltpu.VMEM(square, F32), half, half],
    )
    returned = across(sent)
    halves = [fast(block, BF16)] * 4
    grad_p, grad_q, loss_p, loss_q, ph, plo, qh, qlo = call(
        local_kernel,
        scalars + v(p, q, z, y1, y1s) + [(sent, anywhere)],
        [fast(), fast(), fast(square), fast(square)] + halves,
        [half] * 6 + [pltpu.VMEM(square, F32)] * 4,
    )
    y2s = in_chip(y2[:rows])
    whole = (jax.ShapeDtypeStruct(block, F32), hbm)
    out_scratch = [pltpu.VMEM(block, F32), pltpu.SemaphoreType.DMA((CHUNKS,))]
    image_out, text_out, grad_p, loss_p, loss_q = call(
        second_kernel,
        scalars + v(ph, plo, qh, qlo, y2, y2s, grad_p, grad_q, loss_p, loss_q, q, inv_q),
        [whole, whole, fast(), fast(line), fast(line)],
        [pltpu.VMEM(block, F32)] + [half] * 4 + [pltpu.VMEM(square, F32)] * 2 + out_scratch,
    )
    loss, grad_image, text_gradient = call(
        last_kernel,
        v(grad_p, returned, p, inv_p, loss_p, loss_q) + [(image_out, hbm), (text_out, hbm)],
        [(jax.ShapeDtypeStruct((1, rows), F32), vm), whole, whole],
        out_scratch,
        {6: 1, 7: 2},
    )
    return (loss.reshape(rows), grad_image, text_gradient)


def solution(mesh):
    placed = (P("blk", None), P("blk", None), P(), P())
    return jax.shard_map(
        body,
        mesh=mesh,
        in_specs=placed,
        out_specs=(P("blk"), P("blk", None), P("blk", None)),
        check_vma=False,
    )
```

time: 84.2 us -> 63 us (0.75)
  waiting for transfers between devices: 24 us -> 5.59 us
  Pallas kernels: 0 us -> 16.3 us
  matrix products: 13.2 us -> 0 us
  other arithmetic: 4.75 us -> 0 us
  starting transfers between devices: 39.8 us -> 38.5 us
    ppermute x3, waiting for transfers between devices: 24 us -> 1.98 us  [across(): return lax.ppermute(value, 'blk', pairs)]
    pallas_call x0 -> x6, Pallas kernels: none -> 16.3 us  [call(): pl.pallas_call(kernel, out_shape=[o for o, _ in outs], in_specs=specs, ou...]
    dot_general x15 -> x0, matrix products: 13.2 us -> none  [dot(): lax.dot_general(a, b, (((ca,), (cb,)), ((), ())), precision=HIGH, preferr...]
    ppermute x3, waiting for transfers between devices: 0.01 us -> 3.61 us  [in_chip(): return lax.ppermute(value, 'blk', [(i, i ^ 1) for i in range(count)])]
    reduce_sum x1 -> x0, other arithmetic: 1.96 us -> none  [normalize(): inverse_norm = lax.rsqrt(jnp.sum(raw * raw, axis=-1, keepdims=True) + EPS)]
    select_n x1 -> x0, other arithmetic: 1.82 us -> none  [body(): text_gradient = jnp.where(even, out_q, out_p)]
    ppermute x3, starting transfers between devices: 31.3 us -> 30.2 us  [in_chip(): return lax.ppermute(value, 'blk', [(i, i ^ 1) for i in range(count)])]
  transfers between devices with their start and end apart: 6 -> 6, of which waited for: 2 -> 3; matrix products, arithmetic and copies ran while one was open for 15% -> 0% of each run, Pallas kernels for 0% -> 20%
where the time goes in v3:
time: 63 us; the launch traced here: 62.7 us
  starting transfers between devices  38.5 us (61%)
  Pallas kernels  16.3 us (26%)
  waiting for transfers between devices  5.59 us (9%)
  between operations  2.05 us (3%)
    ppermute x3, starting transfers between devices, in_chip(): return lax.ppermute(value, 'blk', [(i, i ^ 1) for i in range(count)])  30.2 us
    pallas_call x6, Pallas kernels, call(): pl.pallas_call(kernel, out_shape=[o for o, _ in outs], in_specs=specs, ou...  16.3 us
    ppermute x3, starting transfers between devices, across(): return lax.ppermute(value, 'blk', pairs)  8.35 us
    ppermute x3, waiting for transfers between devices, in_chip(): return lax.ppermute(value, 'blk', [(i, i ^ 1) for i in range(count)])  3.61 us
    ppermute x3, waiting for transfers between devices, across(): return lax.ppermute(value, 'blk', pairs)  1.98 us
  transfers between devices with their start and end apart: 6, of which 3 were waited for; matrix products, arithmetic and copies ran while one was open for 0% of the time, Pallas kernels for 20%

profile of v3, /device:TPU:1, one launch (start us, length us, event | category | flops | bytes accessed | tf_op | source)
XLA Modules:
  0.0 62.7 jit_solution(4323845451382336239)
XLA Ops:
  0.6 1.5 %shard_map.67 = (f32[264,1152]{1,0:T(8,128)S(1)}, f32[256,128]{1,0:T(8,128)S(1)}) custom-call(f32[256,1152]{1,0:T(8,128)} %image.3, f32[256,1152]{1,0:T(8,128)} %text.3), custom_call_target="tpu_custom_call" | custom-call | tf_op jit(solution)/shard_map/pallas_call | solution.py:229
  2.1 4.5 %collective-permute-start.1 = (f32[264,1152]{1,0:T(8,128)S(1)}, f32[264,1152]{1,0:T(8,128)S(1)}, u32[]{:S(2)}, u32[]{:S(2)}) collective-permute-start(f32[264,1152]{1,0:T(8,128)S(1)} %get-tuple-element.23.p_ref.p), channel_id=1, source_target_pairs={{0,511},{1,2},{2,1},{3,4},{4,3},{5,6},{6,5},{7,8},{8,7},{9,10},{10... | collective-permute-start | bytes 3649544 | tf_op jit(solution)/shard_map/ppermute | solution.py:22
  6.6 1.5 %shard_map.68 = (f32[256,1152]{1,0:T(8,128)S(1)}, f32[256,128]{1,0:T(8,128)S(1)}) custom-call(f32[256,1152]{1,0:T(8,128)} %image.3, f32[256,1152]{1,0:T(8,128)} %text.3), custom_call_target="tpu_custom_call" | custom-call | tf_op jit(solution)/shard_map/pallas_call | solution.py:229
  8.1 14.4 %collective-permute-start = (f32[256,1152]{1,0:T(8,128)S(1)}, f32[256,1152]{1,0:T(8,128)S(1)}, u32[]{:S(2)}, u32[]{:S(2)}) collective-permute-start(f32[256,1152]{1,0:T(8,128)S(1)} %get-tuple-element.24.q), channel_id=1, source_target_pairs={{0,1},{1,0},{2,3},{3,2},{4,5},{5,4},{6,7},{7,6},{8,9},{9,8},{10,11... | collective-permute-start | bytes 3538952 | tf_op jit(solution)/shard_map/ppermute | solution.py:27
  22.5 2.5 %collective-permute-done.z = f32[256,1152]{1,0:T(8,128)S(1)} collective-permute-done((f32[256,1152]{1,0:T(8,128)S(1)}, f32[256,1152]{1,0:T(8,128)S(1)}, u32[]{:S(2)}, u32[]{:S(2)}) %collective-permute-start) | collective-permute-done | bytes 1179680 | tf_op jit(solution)/shard_map/ppermute | solution.py:27
  25.0 0.1 pad.4
  25.0 1.9 %collective-permute-start.3 = (f32[264,1152]{1,0:T(8,128)S(1)}, f32[264,1152]{1,0:T(8,128)S(1)}, u32[]{:S(2)}, u32[]{:S(2)}) collective-permute-start(f32[264,1152]{1,0:T(8,128)S(1)} %pad.4), channel_id=1, source_target_pairs={{0,511},{1,2},{2,1},{3,4},{4,3},{5,6},{6,5},{7,8},{8,7},{9,10},{10... | collective-permute-start | bytes 3649544 | tf_op jit(solution)/shard_map/ppermute | solution.py:22
  27.0 0.0 collective-permute-done.1.y1
  27.0 0.1 slice.8
  27.1 8.3 %collective-permute-start.2 = (f32[256,1152]{1,0:T(8,128)S(1)}, f32[256,1152]{1,0:T(8,128)S(1)}, u32[]{:S(2)}, u32[]{:S(2)}) collective-permute-start(f32[256,1152]{1,0:T(8,128)S(1)} %slice.8), channel_id=1, source_target_pairs={{0,1},{1,0},{2,3},{3,2},{4,5},{5,4},{6,7},{7,6},{8,9},{9,8},{10,11... | collective-permute-start | bytes 3538952 | tf_op jit(solution)/shard_map/ppermute | solution.py:27
  36.7 1.2 %collective-permute-done.2.y1s = f32[256,1152]{1,0:T(8,128)S(1)} collective-permute-done((f32[256,1152]{1,0:T(8,128)S(1)}, f32[256,1152]{1,0:T(8,128)S(1)}, u32[]{:S(2)}, u32[]{:S(2)}) %collective-permute-start.2) | collective-permute-done | bytes 1179680 | tf_op jit(solution)/shard_map/ppermute | solution.py:27
  37.8 1.5 %shard_map.69.after = f32[264,1152]{1,0:T(8,128)S(1)} custom-call(f32[1]{0:T(128)S(6)} %copy.11.scale, f32[1]{0:T(128)S(6)} %copy.12.shift, f32[264,1152]{1,0:T(8,128)S(1)} %collective-permute-done.1.y1, f32[256,1152]{1,0:T(8,128)S(1)} %collective-permute-done.2.y1s), custom_call_target="tpu_custom_call" | custom-call | tf_op jit(solution)/shard_map/pallas_call | solution.py:229
  39.3 1.9 %collective-permute-start.5 = (f32[264,1152]{1,0:T(8,128)S(1)}, f32[264,1152]{1,0:T(8,128)S(1)}, u32[]{:S(2)}, u32[]{:S(2)}) collective-permute-start(f32[264,1152]{1,0:T(8,128)S(1)} %shard_map.69.after), channel_id=1, source_target_pairs={{0,511},{1,2},{2,1},{3,4},{4,3},{5,6},{6,5},{7,8},{8,7},{9,10},{10... | collective-permute-start | bytes 3649544 | tf_op jit(solution)/shard_map/ppermute | solution.py:22
  41.3 2.0 %collective-permute-done.3.y2 = f32[264,1152]{1,0:T(8,128)S(1)} collective-permute-done((f32[264,1152]{1,0:T(8,128)S(1)}, f32[264,1152]{1,0:T(8,128)S(1)}, u32[]{:S(2)}, u32[]{:S(2)}) %collective-permute-start.3) | collective-permute-done | bytes 1216544 | tf_op jit(solution)/shard_map/ppermute | solution.py:22
  43.2 0.1 slice.9
  43.3 7.5 %collective-permute-start.4 = (f32[256,1152]{1,0:T(8,128)S(1)}, f32[256,1152]{1,0:T(8,128)S(1)}, u32[]{:S(2)}, u32[]{:S(2)}) collective-permute-start(f32[256,1152]{1,0:T(8,128)S(1)} %slice.9), channel_id=1, source_target_pairs={{0,1},{1,0},{2,3},{3,2},{4,5},{5,4},{6,7},{7,6},{8,9},{9,8},{10,11... | collective-permute-start | bytes 3538952 | tf_op jit(solution)/shard_map/ppermute | solution.py:27
  50.8 5.8 %shard_map.70 = (f32[256,1152]{1,0:T(8,128)S(1)}, f32[256,1152]{1,0:T(8,128)S(1)}, f32[256,256]{1,0:T(8,128)S(1)}, f32[256,256]{1,0:T(8,128)S(1)}, bf16[256,1152...) custom-call(f32[1]{0:T(128)S(6)} %copy.11.scale, ...), custom_call_target="tpu_custom_call" | custom-call | tf_op jit(solution)/shard_map/pallas_call | solution.py:229
  56.6 0.0 collective-permute-done.4.y2s
  56.6 4.1 %shard_map.71 = (f32[256,1152]{1,0:T(8,128)}, f32[256,1152]{1,0:T(8,128)}, f32[256,1152]{1,0:T(8,128)S(1)}, f32[8,256]{1,0:T(8,128)S(1)}, f32[8,256]{1,0:T(8,128)S(1)}) custom-call(f32[1]{0:T(128)S(6)} %copy.11.scale, f32[1]{0:T(128)S(6)} %copy.12.shift, bf16[256,1152]{1,0:T(8,128)(2,1)S(1)} %get-tuple-element.25.ph, ...), custom_call_target="tpu_custom_call" | custom-call | tf_op jit(solution)/shard_map/pallas_call | solution.py:229
  60.7 0.0 collective-permute-done.5.returned
  60.7 2.0 %shard_map.72 = (f32[1,256]{1,0:T(1,128)}, f32[256,1152]{1,0:T(8,128)}, f32[256,1152]{1,0:T(8,128)}) custom-call(f32[256,1152]{1,0:T(8,128)S(1)} %get-tuple-element.34.gp_in, f32[264,1152]{1,0:T(8,128)S(1)} %collective-permute-done.5.returned, f32[264,1152]{1,0:T(8,128)S(1)} %get-tuple-element.23.p_ref.p, ...), custom_call_target="tpu_custom_call", output_to_operand_aliasing={{1}: (6, {}), {2}: (7, {})} | custom-call | tf_op jit(solution)/shard_map/pallas_call | solution.py:229
Async XLA Ops:
  2.1 24.9 %collective-permute-start.1 = (f32[264,1152]{1,0:T(8,128)S(1)}, f32[264,1152]{1,0:T(8,128)S(1)}, u32[]{:S(2)}, u32[]{:S(2)}) collective-permute-start(f32[264,1152]{1,0:T(8,128)S(1)} %get-tuple-element.23.p_ref.p), channel_id=1, source_target_pairs={{0,511},{1,2},{2,1},{3,4},{4,3},{5,6},{6,5},{7,8},{8,7},{9,10},{10... | collective-permute-start | bytes 3649544 | tf_op jit(solution)/shard_map/ppermute | solution.py:22
  8.1 16.9 %collective-permute-start = (f32[256,1152]{1,0:T(8,128)S(1)}, f32[256,1152]{1,0:T(8,128)S(1)}, u32[]{:S(2)}, u32[]{:S(2)}) collective-permute-start(f32[256,1152]{1,0:T(8,128)S(1)} %get-tuple-element.24.q), channel_id=1, source_target_pairs={{0,1},{1,0},{2,3},{3,2},{4,5},{5,4},{6,7},{7,6},{8,9},{9,8},{10,11... | collective-permute-start | bytes 3538952 | tf_op jit(solution)/shard_map/ppermute | solution.py:27
  25.0 18.2 %collective-permute-start.3 = (f32[264,1152]{1,0:T(8,128)S(1)}, f32[264,1152]{1,0:T(8,128)S(1)}, u32[]{:S(2)}, u32[]{:S(2)}) collective-permute-start(f32[264,1152]{1,0:T(8,128)S(1)} %pad.4), channel_id=1, source_target_pairs={{0,511},{1,2},{2,1},{3,4},{4,3},{5,6},{6,5},{7,8},{8,7},{9,10},{10... | collective-permute-start | bytes 3649544 | tf_op jit(solution)/shard_map/ppermute | solution.py:22
  27.1 10.8 %collective-permute-start.2 = (f32[256,1152]{1,0:T(8,128)S(1)}, f32[256,1152]{1,0:T(8,128)S(1)}, u32[]{:S(2)}, u32[]{:S(2)}) collective-permute-start(f32[256,1152]{1,0:T(8,128)S(1)} %slice.8), channel_id=1, source_target_pairs={{0,1},{1,0},{2,3},{3,2},{4,5},{5,4},{6,7},{7,6},{8,9},{9,8},{10,11... | collective-permute-start | bytes 3538952 | tf_op jit(solution)/shard_map/ppermute | solution.py:27
  39.3 21.3 %collective-permute-start.5 = (f32[264,1152]{1,0:T(8,128)S(1)}, f32[264,1152]{1,0:T(8,128)S(1)}, u32[]{:S(2)}, u32[]{:S(2)}) collective-permute-start(f32[264,1152]{1,0:T(8,128)S(1)} %shard_map.69.after), channel_id=1, source_target_pairs={{0,511},{1,2},{2,1},{3,4},{4,3},{5,6},{6,5},{7,8},{8,7},{9,10},{10... | collective-permute-start | bytes 3649544 | tf_op jit(solution)/shard_map/ppermute | solution.py:22
  43.3 13.3 %collective-permute-start.4 = (f32[256,1152]{1,0:T(8,128)S(1)}, f32[256,1152]{1,0:T(8,128)S(1)}, u32[]{:S(2)}, u32[]{:S(2)}) collective-permute-start(f32[256,1152]{1,0:T(8,128)S(1)} %slice.9), channel_id=1, source_target_pairs={{0,1},{1,0},{2,3},{3,2},{4,5},{5,4},{6,7},{7,6},{8,9},{9,8},{10,11... | collective-permute-start | bytes 3538952 | tf_op jit(solution)/shard_map/ppermute | solution.py:27

commit v4 on v3

--- a/solution.py
+++ b/solution.py
@@ -13,6 +13,8 @@
 BF16 = jnp.bfloat16
 CHUNKS = 4
 PAD = 8
+COST_Q = 8000000
+COST_OWN = 8000000
 VMEM_LIMIT = 24 * 1024 * 1024
 
 
@@ -100,59 +102,68 @@
         inverse[part] = jnp.broadcast_to(inv, (rows, 128))
 
 
-def middle_kernel(scale, shift, y1, y1s, sent, tile, hi, lo):
-    rows, width = y1s.shape
+def middle_kernel(scale, shift, y1, y1s, sent, tile, yh, yl, sh, sl):
+    rows, width = yh.shape
 
     @step(0)
     def _():
-        hi[...], lo[...] = split(y1s[...])
-        tile[...] = logits(split(y1[:rows]), (hi[...], lo[...]))
+        sh[...], sl[...] = split(y1s[...])
+        yh[...], yl[...] = split(y1[: yh.shape[0]])
+        tile[...] = logits((yh[...], yl[...]), (sh[...], sl[...]))
 
     @step(1)
     def _():
         terms, weight = pair_terms(tile[...], scale[0], shift[0])
-        sent[:rows] = spread(weight, (hi[...], lo[...]))
+        sent[:rows] = spread(weight, (sh[...], sl[...]))
         sent[rows:, :rows] = row_sums(terms)
         sent[rows:, rows:] = jnp.zeros((8, width - rows), F32)
 
 
-def local_kernel(
-    scale, shift, p_ref, q, z, y1, y1s, after, grad_p, grad_q, loss_p, loss_q, ph, plo, qh, qlo,
-    zh, zl, yh, yl, sh, sl, tile_own, tile_z, tile_y, tile_s
+def own_kernel(
+    scale, shift, p, q, z, grad_p, grad_q, loss_p, loss_q, ph, plo, qh, qlo, zh, zl, tile_own, tile_z
 ):
-    rows = q.shape[0]
-
     @step(0)
     def _():
-        ph[...], plo[...] = split(p_ref[:rows])
+        ph[...], plo[...] = split(p[: ph.shape[0]])
         qh[...], qlo[...] = split(q[...])
         tile_own[...] = logits((ph[...], plo[...]), (qh[...], qlo[...]))
         zh[...], zl[...] = split(z[...])
         tile_z[...] = logits((qh[...], qlo[...]), (zh[...], zl[...]))
-        yh[...], yl[...] = split(y1[:rows])
+
+    @step(1)
+    def _():
+        terms, weight = pair_terms(tile_own[...], scale[0], shift[0], own=True)
+        terms_z, weight_z = pair_terms(tile_z[...], scale[0], shift[0])
+        loss_p[...] = terms
+        loss_q[...] = jnp.transpose(terms) + terms_z
+        grad_p[...] = spread(weight, (qh[...], qlo[...]))
+        grad_q[...] = spread(jnp.transpose(weight), (ph[...], plo[...])) + spread(weight_z, (zh[...], zl[...]))
+
+
+def first_kernel(
+    scale, shift, ph, plo, qh, qlo, y1, y1s, y2, gp_in, gq_in, lp_in, lq_in, after,
+    grad_p, grad_q, loss_p, loss_q, yh, yl, sh, sl, wh, wl, tile_y, tile_s, tile_w
+):
+    rows = yh.shape[0]
+
+    @step(0)
+    def _():
+        yh[...], yl[...] = split(y1[: yh.shape[0]])
         tile_y[...] = logits((ph[...], plo[...]), (yh[...], yl[...]))
         sh[...], sl[...] = split(y1s[...])
         tile_s[...] = logits((qh[...], qlo[...]), (sh[...], sl[...]))
+        wh[...], wl[...] = split(y2[:rows])
+        tile_w[...] = logits((ph[...], plo[...]), (wh[...], wl[...]))
 
     @step(1)
     def _():
-        terms_own, weight_own = pair_terms(tile_own[...], scale[0], shift[0], own=True)
         terms_y, weight_y = pair_terms(tile_y[...], scale[0], shift[0])
-        loss_p[...] = terms_own + terms_y
-        tile_own[...] = jnp.transpose(weight_own)
-        grad_p[...] = spread(weight_own, (qh[...], qlo[...])) + spread(weight_y, (yh[...], yl[...]))
-        loss_q[...] = jnp.transpose(terms_own)
-
-    @step(2)
-    def _():
-        terms_z, weight_z = pair_terms(tile_z[...], scale[0], shift[0])
         terms_s, weight_s = pair_terms(tile_s[...], scale[0], shift[0])
-        loss_q[...] += terms_z + terms_s
-        grad_q[...] = (
-            spread(tile_own[...], (ph[...], plo[...]))
-            + spread(weight_z, (zh[...], zl[...]))
-            + spread(weight_s, (sh[...], sl[...]))
-        )
+        terms_w, weight_w = pair_terms(tile_w[...], scale[0], shift[0])
+        loss_p[...] = row_sums(lp_in[...] + terms_y + terms_w)
+        loss_q[...] = lq_in[...] + terms_s
+        grad_p[...] = gp_in[...] + spread(weight_y, (yh[...], yl[...])) + spread(weight_w, (wh[...], wl[...]))
+        grad_q[...] = gq_in[...] + spread(weight_s, (sh[...], sl[...]))
 
 
 def restored(unit, inverse, grad):
@@ -184,26 +195,19 @@
 
 
 def second_kernel(
-    scale, shift, ph, plo, qh, qlo, y2, y2s, gp_in, gq_in, lp_in, lq_in, q, inv_q,
-    image_out, text_out, grad_p, loss_p, loss_q, grad_q, yh, yl, sh, sl, tile_y, tile_s, result, sem
+    scale, shift, qh, qlo, y2s, gq_in, lq_in, q, inv_q,
+    image_out, text_out, loss_q, grad_q, sh, sl, tile_s, result, sem
 ):
-    rows = q.shape[0]
-
     @step(0)
     def _():
-        yh[...], yl[...] = split(y2[:rows])
-        tile_y[...] = logits((ph[...], plo[...]), (yh[...], yl[...]))
         sh[...], sl[...] = split(y2s[...])
         tile_s[...] = logits((qh[...], qlo[...]), (sh[...], sl[...]))
 
     @step(1)
     def _():
-        terms_s, weight_s = pair_terms(tile_s[...], scale[0], shift[0])
-        grad_q[...] = gq_in[...] + spread(weight_s, (sh[...], sl[...]))
-        terms_y, weight_y = pair_terms(tile_y[...], scale[0], shift[0])
-        grad_p[...] = gp_in[...] + spread(weight_y, (yh[...], yl[...]))
-        loss_p[...] = row_sums(lp_in[...] + terms_y)
-        loss_q[...] = row_sums(lq_in[...] + terms_s)
+        terms, weight = pair_terms(tile_s[...], scale[0], shift[0])
+        grad_q[...] = gq_in[...] + spread(weight, (sh[...], sl[...]))
+        loss_q[...] = row_sums(lq_in[...] + terms)
 
     odd = lax.rem(lax.axis_index("blk"), 2) == 1
     finish(q, inv_q, lambda part: grad_q[part], image_out, text_out, result, sem, odd)
@@ -221,7 +225,7 @@
     )
 
 
-def call(kernel, ins, outs, scratch=(), aliases=None):
+def call(kernel, ins, outs, scratch=(), aliases=None, cost=0):
     arrays, specs = [], []
     for array, place in ins:
         specs.append(pl.BlockSpec(memory_space=place))
@@ -234,7 +238,7 @@
         scratch_shapes=list(scratch),
         input_output_aliases=aliases or {},
         compiler_params=pltpu.CompilerParams(vmem_limit_bytes=VMEM_LIMIT),
-        cost_estimate=pl.CostEstimate(flops=0, transcendentals=0, bytes_accessed=0),
+        cost_estimate=pl.CostEstimate(flops=0, transcendentals=0, bytes_accessed=cost),
     )(*arrays)
 
 
@@ -251,43 +255,54 @@
     def v(*arrays):
         return [(a, vm) for a in arrays]
 
-    def pick(odd_takes, taken):
+    def pick(odd_takes, taken, cost):
         return call(
             functools.partial(pick_kernel, odd_takes),
             [(picture_vectors, hbm), (caption_vectors, hbm)],
             [fast((taken, width)), fast((rows, 128))],
             [pltpu.VMEM(block, F32), pltpu.SemaphoreType.DMA((CHUNKS,))],
+            cost=cost,
         )
 
     line, square, half = (8, rows), (rows, rows), pltpu.VMEM(block, BF16)
-    p, inv_p = pick(1, rows + PAD)
+    tile = pltpu.VMEM(square, F32)
+    p, inv_p = pick(1, rows + PAD, 0)
     y1 = across(p)
-    q, inv_q = pick(0, rows)
+    q, inv_q = pick(0, rows, COST_Q)
     z = in_chip(q)
     y2 = across(jnp.pad(z, ((0, PAD), (0, 0))))
+    grad_p, grad_q, loss_p, loss_q, ph, plo, qh, qlo = call(
+        own_kernel,
+        scalars + v(p, q, z),
+        [fast(), fast(), fast(square), fast(square)] + [fast(block, BF16)] * 4,
+        [half] * 2 + [tile] * 2,
+        cost=COST_OWN,
+    )
+    y1, grad_p = lax.optimization_barrier((y1, grad_p))
     y1s = in_chip(y1[:rows])
     (sent,) = call(
         middle_kernel,
         scalars + v(y1, y1s),
         [fast((rows + 8, width))],
-        [pltpu.VMEM(square, F32), half, half],
+        [tile] + [half] * 4,
     )
     returned = across(sent)
-    halves = [fast(block, BF16)] * 4
-    grad_p, grad_q, loss_p, loss_q, ph, plo, qh, qlo = call(
-        local_kernel,
-        scalars + v(p, q, z, y1, y1s) + [(sent, anywhere)],
-        [fast(), fast(), fast(square), fast(square)] + halves,
-        [half] * 6 + [pltpu.VMEM(square, F32)] * 4,
-    )
     y2s = in_chip(y2[:rows])
+    grad_p, grad_q, loss_p, loss_q = call(
+        first_kernel,
+        scalars
+        + v(ph, plo, qh, qlo, y1, y1s, y2, grad_p, grad_q, loss_p, loss_q)
+        + [(sent, anywhere)],
+        [fast(), fast(), fast(line), fast(square)],
+        [half] * 6 + [tile] * 3,
+    )
     whole = (jax.ShapeDtypeStruct(block, F32), hbm)
     out_scratch = [pltpu.VMEM(block, F32), pltpu.SemaphoreType.DMA((CHUNKS,))]
-    image_out, text_out, grad_p, loss_p, loss_q = call(
+    image_out, text_out, loss_q = call(
         second_kernel,
-        scalars + v(ph, plo, qh, qlo, y2, y2s, grad_p, grad_q, loss_p, loss_q, q, inv_q),
-        [whole, whole, fast(), fast(line), fast(line)],
-        [pltpu.VMEM(block, F32)] + [half] * 4 + [pltpu.VMEM(square, F32)] * 2 + out_scratch,
+        scalars + v(qh, qlo, y2s, grad_q, loss_q, q, inv_q),
+        [whole, whole, fast(line)],
+        [pltpu.VMEM(block, F32)] + [half] * 2 + [tile] + out_scratch,
     )
     loss, grad_image, text_gradient = call(
         last_kernel,

time: 63 us -> 60.1 us (0.954)
  starting transfers between devices: 38.5 us -> 35.3 us
    ppermute x3, starting transfers between devices: 30.2 us -> 27 us  [in_chip(): return lax.ppermute(value, 'blk', [(i, i ^ 1) for i in range(count)])]
    pallas_call x6 -> x7, Pallas kernels: 16.3 us -> 16.6 us  [call(): pl.pallas_call(kernel, out_shape=[o for o, _ in outs], in_specs=specs, ou...]
  transfers between devices with their start and end apart: 6 -> 6, of which waited for: 3 -> 3; matrix products, arithmetic and copies ran while one was open for 0% -> 0% of each run, Pallas kernels for 20% -> 22%
where the time goes in v4:
time: 60.1 us; the launch traced here: 59.7 us
  starting transfers between devices  35.3 us (59%)
  Pallas kernels  16.6 us (28%)
  waiting for transfers between devices  5.55 us (9%)
  between operations  2.04 us (3%)
    ppermute x3, starting transfers between devices, in_chip(): return lax.ppermute(value, 'blk', [(i, i ^ 1) for i in range(count)])  27 us
    pallas_call x7, Pallas kernels, call(): pl.pallas_call(kernel, out_shape=[o for o, _ in outs], in_specs=specs, ou...  16.6 us
    ppermute x3, starting transfers between devices, across(): return lax.ppermute(value, 'blk', pairs)  8.35 us
    ppermute x3, waiting for transfers between devices, in_chip(): return lax.ppermute(value, 'blk', [(i, i ^ 1) for i in range(count)])  3.61 us
    ppermute x3, waiting for transfers between devices, across(): return lax.ppermute(value, 'blk', pairs)  1.94 us
  transfers between devices with their start and end apart: 6, of which 3 were waited for; matrix products, arithmetic and copies ran while one was open for 0% of the time, Pallas kernels for 22%

profile of v4, /device:TPU:1, one launch (start us, length us, event | category | flops | bytes accessed | tf_op | source)
XLA Modules:
  0.0 59.7 jit_solution(16757367946289636831)
XLA Ops:
  0.6 1.5 %shard_map.67 = (f32[264,1152]{1,0:T(8,128)S(1)}, f32[256,128]{1,0:T(8,128)S(1)}) custom-call(f32[256,1152]{1,0:T(8,128)} %image.3, f32[256,1152]{1,0:T(8,128)} %text.3), custom_call_target="tpu_custom_call" | custom-call | tf_op jit(solution)/shard_map/pallas_call | solution.py:233
  2.1 4.5 %collective-permute-start.1 = (f32[264,1152]{1,0:T(8,128)S(1)}, f32[264,1152]{1,0:T(8,128)S(1)}, u32[]{:S(2)}, u32[]{:S(2)}) collective-permute-start(f32[264,1152]{1,0:T(8,128)S(1)} %get-tuple-element.27.p), channel_id=1, source_target_pairs={{0,511},{1,2},{2,1},{3,4},{4,3},{5,6},{6,5},{7,8},{8,7},{9,10},{10... | collective-permute-start | bytes 3649544 | tf_op jit(solution)/shard_map/ppermute | solution.py:24
  6.6 1.5 %shard_map.68 = (f32[256,1152]{1,0:T(8,128)S(1)}, f32[256,128]{1,0:T(8,128)S(1)}) custom-call(f32[256,1152]{1,0:T(8,128)} %image.3, f32[256,1152]{1,0:T(8,128)} %text.3), custom_call_target="tpu_custom_call" | custom-call | bytes 8000000 | tf_op jit(solution)/shard_map/pallas_call | solution.py:233
  8.1 14.4 %collective-permute-start = (f32[256,1152]{1,0:T(8,128)S(1)}, f32[256,1152]{1,0:T(8,128)S(1)}, u32[]{:S(2)}, u32[]{:S(2)}) collective-permute-start(f32[256,1152]{1,0:T(8,128)S(1)} %get-tuple-element.28.q), channel_id=1, source_target_pairs={{0,1},{1,0},{2,3},{3,2},{4,5},{5,4},{6,7},{7,6},{8,9},{9,8},{10,11... | collective-permute-start | bytes 3538952 | tf_op jit(solution)/shard_map/ppermute | solution.py:29
  23.8 1.2 %collective-permute-done.z = f32[256,1152]{1,0:T(8,128)S(1)} collective-permute-done((f32[256,1152]{1,0:T(8,128)S(1)}, f32[256,1152]{1,0:T(8,128)S(1)}, u32[]{:S(2)}, u32[]{:S(2)}) %collective-permute-start) | collective-permute-done | bytes 1179680 | tf_op jit(solution)/shard_map/ppermute | solution.py:29
  25.0 0.1 pad.4
  25.0 1.9 %collective-permute-start.3 = (f32[264,1152]{1,0:T(8,128)S(1)}, f32[264,1152]{1,0:T(8,128)S(1)}, u32[]{:S(2)}, u32[]{:S(2)}) collective-permute-start(f32[264,1152]{1,0:T(8,128)S(1)} %pad.4), channel_id=1, source_target_pairs={{0,511},{1,2},{2,1},{3,4},{4,3},{5,6},{6,5},{7,8},{8,7},{9,10},{10... | collective-permute-start | bytes 3649544 | tf_op jit(solution)/shard_map/ppermute | solution.py:24
  27.0 3.3 %shard_map.69 = (f32[256,1152]{1,0:T(8,128)S(1)}, f32[256,1152]{1,0:T(8,128)S(1)}, f32[256,256]{1,0:T(8,128)S(1)}, f32[256,256]{1,0:T(8,128)S(1)}, bf16[256,1152...) custom-call(f32[1]{0:T(128)S(6)} %copy.11.scale, ...), custom_call_target="tpu_custom_call" | custom-call | bytes 8000000 | tf_op jit(solution)/shard_map/pallas_call | solution.py:233
  30.2 0.0 collective-permute-done.1.y1
  30.2 0.1 slice.6
  30.3 5.0 %collective-permute-start.2 = (f32[256,1152]{1,0:T(8,128)S(1)}, f32[256,1152]{1,0:T(8,128)S(1)}, u32[]{:S(2)}, u32[]{:S(2)}) collective-permute-start(f32[256,1152]{1,0:T(8,128)S(1)} %slice.6), channel_id=1, source_target_pairs={{0,1},{1,0},{2,3},{3,2},{4,5},{5,4},{6,7},{7,6},{8,9},{9,8},{10,11... | collective-permute-start | bytes 3538952 | tf_op jit(solution)/shard_map/ppermute | solution.py:29
  35.4 2.5 %collective-permute-done.2.y1s = f32[256,1152]{1,0:T(8,128)S(1)} collective-permute-done((f32[256,1152]{1,0:T(8,128)S(1)}, f32[256,1152]{1,0:T(8,128)S(1)}, u32[]{:S(2)}, u32[]{:S(2)}) %collective-permute-start.2) | collective-permute-done | bytes 1179680 | tf_op jit(solution)/shard_map/ppermute | solution.py:29
  37.8 1.6 %shard_map.70.after = f32[264,1152]{1,0:T(8,128)S(1)} custom-call(f32[1]{0:T(128)S(6)} %copy.11.scale, f32[1]{0:T(128)S(6)} %copy.12.shift, f32[264,1152]{1,0:T(8,128)S(1)} %collective-permute-done.1.y1, f32[256,1152]{1,0:T(8,128)S(1)} %collective-permute-done.2.y1s), custom_call_target="tpu_custom_call" | custom-call | tf_op jit(solution)/shard_map/pallas_call | solution.py:233
  39.4 1.9 %collective-permute-start.4 = (f32[264,1152]{1,0:T(8,128)S(1)}, f32[264,1152]{1,0:T(8,128)S(1)}, u32[]{:S(2)}, u32[]{:S(2)}) collective-permute-start(f32[264,1152]{1,0:T(8,128)S(1)} %shard_map.70.after), channel_id=1, source_target_pairs={{0,511},{1,2},{2,1},{3,4},{4,3},{5,6},{6,5},{7,8},{8,7},{9,10},{10... | collective-permute-start | bytes 3649544 | tf_op jit(solution)/shard_map/ppermute | solution.py:24
  41.3 1.9 %collective-permute-done.3.y2 = f32[264,1152]{1,0:T(8,128)S(1)} collective-permute-done((f32[264,1152]{1,0:T(8,128)S(1)}, f32[264,1152]{1,0:T(8,128)S(1)}, u32[]{:S(2)}, u32[]{:S(2)}) %collective-permute-start.3) | collective-permute-done | bytes 1216544 | tf_op jit(solution)/shard_map/ppermute | solution.py:24
  43.2 0.1 slice.8
  43.3 7.5 %collective-permute-start.5 = (f32[256,1152]{1,0:T(8,128)S(1)}, f32[256,1152]{1,0:T(8,128)S(1)}, u32[]{:S(2)}, u32[]{:S(2)}) collective-permute-start(f32[256,1152]{1,0:T(8,128)S(1)} %slice.8), channel_id=1, source_target_pairs={{0,1},{1,0},{2,3},{3,2},{4,5},{5,4},{6,7},{7,6},{8,9},{9,8},{10,11... | collective-permute-start | bytes 3538952 | tf_op jit(solution)/shard_map/ppermute | solution.py:29
  50.9 4.0 %shard_map.71 = (f32[256,1152]{1,0:T(8,128)S(1)}, f32[256,1152]{1,0:T(8,128)S(1)}, f32[8,256]{1,0:T(8,128)S(1)}, f32[256,256]{1,0:T(8,128)S(1)}) custom-call(f32[1]{0:T(128)S(6)} %copy.11.scale, f32[1]{0:T(128)S(6)} %copy.12.shift, bf16[256,1152]{1,0:T(8,128)(2,1)S(1)} %get-tuple-element.29.ph, bf16[256,1152]{1,0:T(8,128)(2,1)S(1)} %get-tuple-element.30.plo, ...), custom_call_target="tpu_custom_call" | custom-call | tf_op jit(solution)/shard_map/pallas_call | solution.py:233
  54.8 0.0 collective-permute-done.5.y2s
  54.8 2.9 %shard_map.72 = (f32[256,1152]{1,0:T(8,128)}, f32[256,1152]{1,0:T(8,128)}, f32[8,256]{1,0:T(8,128)S(1)}) custom-call(f32[1]{0:T(128)S(6)} %copy.11.scale, f32[1]{0:T(128)S(6)} %copy.12.shift, bf16[256,1152]{1,0:T(8,128)(2,1)S(1)} %get-tuple-element.31.qh, bf16[256,1152]{1,0:T(8,128)(2,1)S(1)} %get-tuple-element.32.qlo, ...), custom_call_target="tpu_custom_call" | custom-call | tf_op jit(solution)/shard_map/pallas_call | solution.py:233
  57.7 0.0 collective-permute-done.4.returned
  57.8 2.0 %shard_map.73 = (f32[1,256]{1,0:T(1,128)}, f32[256,1152]{1,0:T(8,128)}, f32[256,1152]{1,0:T(8,128)}) custom-call(f32[256,1152]{1,0:T(8,128)S(1)} %get-tuple-element.39.gp_in, f32[264,1152]{1,0:T(8,128)S(1)} %collective-permute-done.4.returned, f32[264,1152]{1,0:T(8,128)S(1)} %get-tuple-element.27.p, ...), custom_call_target="tpu_custom_call", output_to_operand_aliasing={{1}: (6, {}), {2}: (7, {})} | custom-call | tf_op jit(solution)/shard_map/pallas_call | solution.py:233
Async XLA Ops:
  2.1 28.1 %collective-permute-start.1 = (f32[264,1152]{1,0:T(8,128)S(1)}, f32[264,1152]{1,0:T(8,128)S(1)}, u32[]{:S(2)}, u32[]{:S(2)}) collective-permute-start(f32[264,1152]{1,0:T(8,128)S(1)} %get-tuple-element.27.p), channel_id=1, source_target_pairs={{0,511},{1,2},{2,1},{3,4},{4,3},{5,6},{6,5},{7,8},{8,7},{9,10},{10... | collective-permute-start | bytes 3649544 | tf_op jit(solution)/shard_map/ppermute | solution.py:24
  8.1 16.9 %collective-permute-start = (f32[256,1152]{1,0:T(8,128)S(1)}, f32[256,1152]{1,0:T(8,128)S(1)}, u32[]{:S(2)}, u32[]{:S(2)}) collective-permute-start(f32[256,1152]{1,0:T(8,128)S(1)} %get-tuple-element.28.q), channel_id=1, source_target_pairs={{0,1},{1,0},{2,3},{3,2},{4,5},{5,4},{6,7},{7,6},{8,9},{9,8},{10,11... | collective-permute-start | bytes 3538952 | tf_op jit(solution)/shard_map/ppermute | solution.py:29
  25.0 18.2 %collective-permute-start.3 = (f32[264,1152]{1,0:T(8,128)S(1)}, f32[264,1152]{1,0:T(8,128)S(1)}, u32[]{:S(2)}, u32[]{:S(2)}) collective-permute-start(f32[264,1152]{1,0:T(8,128)S(1)} %pad.4), channel_id=1, source_target_pairs={{0,511},{1,2},{2,1},{3,4},{4,3},{5,6},{6,5},{7,8},{8,7},{9,10},{10... | collective-permute-start | bytes 3649544 | tf_op jit(solution)/shard_map/ppermute | solution.py:24
  30.3 7.5 %collective-permute-start.2 = (f32[256,1152]{1,0:T(8,128)S(1)}, f32[256,1152]{1,0:T(8,128)S(1)}, u32[]{:S(2)}, u32[]{:S(2)}) collective-permute-start(f32[256,1152]{1,0:T(8,128)S(1)} %slice.6), channel_id=1, source_target_pairs={{0,1},{1,0},{2,3},{3,2},{4,5},{5,4},{6,7},{7,6},{8,9},{9,8},{10,11... | collective-permute-start | bytes 3538952 | tf_op jit(solution)/shard_map/ppermute | solution.py:29
  39.4 18.4 %collective-permute-start.4 = (f32[264,1152]{1,0:T(8,128)S(1)}, f32[264,1152]{1,0:T(8,128)S(1)}, u32[]{:S(2)}, u32[]{:S(2)}) collective-permute-start(f32[264,1152]{1,0:T(8,128)S(1)} %shard_map.70.after), channel_id=1, source_target_pairs={{0,511},{1,2},{2,1},{3,4},{4,3},{5,6},{6,5},{7,8},{8,7},{9,10},{10... | collective-permute-start | bytes 3649544 | tf_op jit(solution)/shard_map/ppermute | solution.py:24
  43.3 11.5 %collective-permute-start.5 = (f32[256,1152]{1,0:T(8,128)S(1)}, f32[256,1152]{1,0:T(8,128)S(1)}, u32[]{:S(2)}, u32[]{:S(2)}) collective-permute-start(f32[256,1152]{1,0:T(8,128)S(1)} %slice.8), channel_id=1, source_target_pairs={{0,1},{1,0},{2,3},{3,2},{4,5},{5,4},{6,7},{7,6},{8,9},{9,8},{10,11... | collective-permute-start | bytes 3538952 | tf_op jit(solution)/shard_map/ppermute | solution.py:29

commit v5 on v4

--- a/solution.py
+++ b/solution.py
@@ -140,30 +140,56 @@
         grad_q[...] = spread(jnp.transpose(weight), (ph[...], plo[...])) + spread(weight_z, (zh[...], zl[...]))
 
 
-def first_kernel(
-    scale, shift, ph, plo, qh, qlo, y1, y1s, y2, gp_in, gq_in, lp_in, lq_in, after,
-    grad_p, grad_q, loss_p, loss_q, yh, yl, sh, sl, wh, wl, tile_y, tile_s, tile_w
-):
-    rows = yh.shape[0]
-
-    @step(0)
-    def _():
+def add_first(scale, shift, ph, plo, qh, qlo, y1, y1s, gp_in, gq_in, lp_in, lq_in, grad_p, grad_q, loss_p, loss_q, scratch):
+    yh, yl, sh, sl, tile_y, tile_s = scratch
+
+    def logit_part():
         yh[...], yl[...] = split(y1[: yh.shape[0]])
         tile_y[...] = logits((ph[...], plo[...]), (yh[...], yl[...]))
         sh[...], sl[...] = split(y1s[...])
         tile_s[...] = logits((qh[...], qlo[...]), (sh[...], sl[...]))
-        wh[...], wl[...] = split(y2[:rows])
-        tile_w[...] = logits((ph[...], plo[...]), (wh[...], wl[...]))
-
-    @step(1)
-    def _():
+
+    def gradient_part():
         terms_y, weight_y = pair_terms(tile_y[...], scale[0], shift[0])
         terms_s, weight_s = pair_terms(tile_s[...], scale[0], shift[0])
-        terms_w, weight_w = pair_terms(tile_w[...], scale[0], shift[0])
-        loss_p[...] = row_sums(lp_in[...] + terms_y + terms_w)
+        loss_p[...] = lp_in[...] + terms_y
         loss_q[...] = lq_in[...] + terms_s
-        grad_p[...] = gp_in[...] + spread(weight_y, (yh[...], yl[...])) + spread(weight_w, (wh[...], wl[...]))
+        grad_p[...] = gp_in[...] + spread(weight_y, (yh[...], yl[...]))
         grad_q[...] = gq_in[...] + spread(weight_s, (sh[...], sl[...]))
+
+    return logit_part, gradient_part
+
+
+def odd_first_kernel(
+    scale, shift, ph, plo, qh, qlo, y1, y1s, gp_in, gq_in, lp_in, lq_in, after, grad_p, grad_q, loss_p, loss_q, *scratch
+):
+    parts = add_first(
+        scale, shift, ph, plo, qh, qlo, y1, y1s, gp_in, gq_in, lp_in, lq_in, grad_p, grad_q, loss_p, loss_q, scratch
+    )
+    for part in parts:
+        pl.when(lax.rem(lax.axis_index("blk"), 2) == 1)(part)
+
+
+def even_first_kernel(
+    scale, shift, ph, plo, qh, qlo, y1, y1s, y2, gp_in, gq_in, lp_in, lq_in, grad_p, grad_q, loss_p, loss_q,
+    wh, wl, tile_w, *scratch
+):
+    parts = add_first(
+        scale, shift, ph, plo, qh, qlo, y1, y1s, gp_in, gq_in, lp_in, lq_in, grad_p, grad_q, loss_p, loss_q, scratch
+    )
+    for part in parts:
+        pl.when(lax.rem(lax.axis_index("blk"), 2) == 0)(part)
+
+    @step(0)
+    def _():
+        wh[...], wl[...] = split(y2[: wh.shape[0]])
+        tile_w[...] = logits((ph[...], plo[...]), (wh[...], wl[...]))
+
+    @step(1)
+    def _():
+        terms, weight = pair_terms(tile_w[...], scale[0], shift[0])
+        loss_p[...] = lp_in[...] + terms
+        grad_p[...] = gp_in[...] + spread(weight, (wh[...], wl[...]))
 
 
 def restored(unit, inverse, grad):
@@ -195,34 +221,47 @@
 
 
 def second_kernel(
-    scale, shift, qh, qlo, y2s, gq_in, lq_in, q, inv_q,
-    image_out, text_out, loss_q, grad_q, sh, sl, tile_s, result, sem
+    scale, shift, qh, qlo, y2s, gq_in, lq_in, lp_in, q, inv_q,
+    image_out, text_out, loss_q, loss_p, sh, sl, tile_s, result, sem
 ):
     @step(0)
     def _():
         sh[...], sl[...] = split(y2s[...])
         tile_s[...] = logits((qh[...], qlo[...]), (sh[...], sl[...]))
 
-    @step(1)
-    def _():
-        terms, weight = pair_terms(tile_s[...], scale[0], shift[0])
-        grad_q[...] = gq_in[...] + spread(weight, (sh[...], sl[...]))
-        loss_q[...] = row_sums(lq_in[...] + terms)
-
     odd = lax.rem(lax.axis_index("blk"), 2) == 1
-    finish(q, inv_q, lambda part: grad_q[part], image_out, text_out, result, sem, odd)
+    rows = result.shape[0] // 2
+    for h in range(2):
+        part = pl.ds(h * rows, rows)
+
+        @step(1 + h)
+        def _():
+            terms, weight = pair_terms(tile_s[part], scale[0], shift[0])
+            grad = gq_in[part] + spread(weight, (sh[...], sl[...]))
+            result[part] = restored(q[part], inv_q[part][:, :1], grad)
+            tile_s[part] = lq_in[part] + terms
+            put(result, image_out, text_out, odd, sem, h, rows)
+
+    loss_q[...] = row_sums(tile_s[...])
+    loss_p[...] = row_sums(lp_in[...])
+    for h in range(2):
+        part = pl.ds(h * rows, rows)
+        pltpu.make_async_copy(result.at[part], image_out.at[part], sem.at[h]).wait()
 
 
 def last_kernel(
-    gp_in, returned, p, inv_p, loss_p, loss_q, image_in, text_in, loss, image_out, text_out, result, sem
+    gp_in, returned, p, inv_p, loss_p, loss_q, image_in, text_in, loss, image_out, text_out, result, sem, line, line_sem
 ):
     rows = result.shape[0]
     even = lax.rem(lax.axis_index("blk"), 2) == 0
     total = jnp.where(even, loss_p[:1] + returned[rows : rows + 1, :rows], loss_q[:1])
-    loss[...] = total * (1.0 / HOPS)
+    line[...] = total * (1.0 / HOPS)
+    copy = pltpu.make_async_copy(line, loss, line_sem)
+    copy.start()
     finish(
         p, inv_p, lambda part: gp_in[part] + returned[part], image_out, text_out, result, sem, even
     )
+    copy.wait()
 
 
 def call(kernel, ins, outs, scratch=(), aliases=None, cost=0):
@@ -287,28 +326,38 @@
         [tile] + [half] * 4,
     )
     returned = across(sent)
+    state = [grad_p, grad_q, loss_p, loss_q]
+    outs = [fast(), fast(), fast(square), fast(square)]
+    scratch = [half] * 4 + [tile] * 2
+    state = call(
+        odd_first_kernel,
+        scalars + v(ph, plo, qh, qlo, y1, y1s, *state) + [(sent, anywhere)],
+        outs,
+        scratch,
+        {8 + i: i for i in range(4)},
+    )
+    y2, state = lax.optimization_barrier((y2, state))
     y2s = in_chip(y2[:rows])
     grad_p, grad_q, loss_p, loss_q = call(
-        first_kernel,
-        scalars
-        + v(ph, plo, qh, qlo, y1, y1s, y2, grad_p, grad_q, loss_p, loss_q)
-        + [(sent, anywhere)],
-        [fast(), fast(), fast(line), fast(square)],
-        [half] * 6 + [tile] * 3,
+        even_first_kernel,
+        scalars + v(ph, plo, qh, qlo, y1, y1s, y2, *state),
+        outs,
+        [half, half, tile] + scratch,
+        {9 + i: i for i in range(4)},
     )
     whole = (jax.ShapeDtypeStruct(block, F32), hbm)
     out_scratch = [pltpu.VMEM(block, F32), pltpu.SemaphoreType.DMA((CHUNKS,))]
-    image_out, text_out, loss_q = call(
+    image_out, text_out, loss_q, loss_p = call(
         second_kernel,
-        scalars + v(qh, qlo, y2s, grad_q, loss_q, q, inv_q),
-        [whole, whole, fast(line)],
-        [pltpu.VMEM(block, F32)] + [half] * 2 + [tile] + out_scratch,
+        scalars + v(qh, qlo, y2s, grad_q, loss_q, loss_p, q, inv_q),
+        [whole, whole, fast(line), fast(line)],
+        [half] * 2 + [tile] + out_scratch,
     )
     loss, grad_image, text_gradient = call(
         last_kernel,
         v(grad_p, returned, p, inv_p, loss_p, loss_q) + [(image_out, hbm), (text_out, hbm)],
-        [(jax.ShapeDtypeStruct((1, rows), F32), vm), whole, whole],
-        out_scratch,
+        [(jax.ShapeDtypeStruct((1, rows), F32), hbm), whole, whole],
+        out_scratch + [pltpu.VMEM((1, rows), F32), pltpu.SemaphoreType.DMA],
         {6: 1, 7: 2},
     )
     return (loss.reshape(rows), grad_image, text_gradient)

time: 60.1 us -> 59.5 us (0.990)
  starting transfers between devices: 35.3 us -> 33 us
  waiting for transfers between devices: 5.55 us -> 6.83 us
    ppermute x3, starting transfers between devices: 27 us -> 24.3 us  [in_chip(): return lax.ppermute(value, 'blk', [(i, i ^ 1) for i in range(count)])]
    ppermute x3, waiting for transfers between devices: 3.61 us -> 5.5 us  [in_chip(): return lax.ppermute(value, 'blk', [(i, i ^ 1) for i in range(count)])]
    pallas_call x7 -> x8, Pallas kernels: 16.6 us -> 16.9 us  [call(): pl.pallas_call(kernel, out_shape=[o for o, _ in outs], in_specs=specs, ou...]
  transfers between devices with their start and end apart: 6 -> 6, of which waited for: 3 -> 4; matrix products, arithmetic and copies ran while one was open for 0% -> 0% of each run, Pallas kernels for 22% -> 24%
where the time goes in v5:
time: 59.5 us; the launch traced here: 59.2 us
  starting transfers between devices  33 us (55%)
  Pallas kernels  16.9 us (28%)
  waiting for transfers between devices  6.83 us (11%)
  between operations  2.22 us (4%)
    ppermute x3, starting transfers between devices, in_chip(): return lax.ppermute(value, 'blk', [(i, i ^ 1) for i in range(count)])  24.3 us
    pallas_call x8, Pallas kernels, call(): pl.pallas_call(kernel, out_shape=[o for o, _ in outs], in_specs=specs, ou...  16.9 us
    ppermute x3, starting transfers between devices, across(): return lax.ppermute(value, 'blk', pairs)  8.62 us
    ppermute x3, waiting for transfers between devices, in_chip(): return lax.ppermute(value, 'blk', [(i, i ^ 1) for i in range(count)])  5.5 us
    ppermute x3, waiting for transfers between devices, across(): return lax.ppermute(value, 'blk', pairs)  1.34 us
  transfers between devices with their start and end apart: 6, of which 4 were waited for; matrix products, arithmetic and copies ran while one was open for 0% of the time, Pallas kernels for 24%

profile of v5, /device:TPU:1, one launch (start us, length us, event | category | flops | bytes accessed | tf_op | source)
XLA Modules:
  0.0 59.2 jit_solution(5842616595999711980)
XLA Ops:
  0.6 1.5 %shard_map.67 = (f32[264,1152]{1,0:T(8,128)S(1)}, f32[256,128]{1,0:T(8,128)S(1)}) custom-call(f32[256,1152]{1,0:T(8,128)} %image.3, f32[256,1152]{1,0:T(8,128)} %text.3), custom_call_target="tpu_custom_call" | custom-call | tf_op jit(solution)/shard_map/pallas_call | solution.py:272
  2.1 4.5 %collective-permute-start.1 = (f32[264,1152]{1,0:T(8,128)S(1)}, f32[264,1152]{1,0:T(8,128)S(1)}, u32[]{:S(2)}, u32[]{:S(2)}) collective-permute-start(f32[264,1152]{1,0:T(8,128)S(1)} %get-tuple-element.37.p), channel_id=1, source_target_pairs={{0,511},{1,2},{2,1},{3,4},{4,3},{5,6},{6,5},{7,8},{8,7},{9,10},{10... | collective-permute-start | bytes 3649544 | tf_op jit(solution)/shard_map/ppermute | solution.py:24
  6.6 1.5 %shard_map.68 = (f32[256,1152]{1,0:T(8,128)S(1)}, f32[256,128]{1,0:T(8,128)S(1)}) custom-call(f32[256,1152]{1,0:T(8,128)} %image.3, f32[256,1152]{1,0:T(8,128)} %text.3), custom_call_target="tpu_custom_call" | custom-call | bytes 8000000 | tf_op jit(solution)/shard_map/pallas_call | solution.py:272
  8.1 14.4 %collective-permute-start = (f32[256,1152]{1,0:T(8,128)S(1)}, f32[256,1152]{1,0:T(8,128)S(1)}, u32[]{:S(2)}, u32[]{:S(2)}) collective-permute-start(f32[256,1152]{1,0:T(8,128)S(1)} %get-tuple-element.38.q), channel_id=1, source_target_pairs={{0,1},{1,0},{2,3},{3,2},{4,5},{5,4},{6,7},{7,6},{8,9},{9,8},{10,11... | collective-permute-start | bytes 3538952 | tf_op jit(solution)/shard_map/ppermute | solution.py:29
  22.5 2.5 %collective-permute-done.z = f32[256,1152]{1,0:T(8,128)S(1)} collective-permute-done((f32[256,1152]{1,0:T(8,128)S(1)}, f32[256,1152]{1,0:T(8,128)S(1)}, u32[]{:S(2)}, u32[]{:S(2)}) %collective-permute-start) | collective-permute-done | bytes 1179680 | tf_op jit(solution)/shard_map/ppermute | solution.py:29
  25.0 0.1 pad.4
  25.0 1.9 %collective-permute-start.3 = (f32[264,1152]{1,0:T(8,128)S(1)}, f32[264,1152]{1,0:T(8,128)S(1)}, u32[]{:S(2)}, u32[]{:S(2)}) collective-permute-start(f32[264,1152]{1,0:T(8,128)S(1)} %pad.4), channel_id=1, source_target_pairs={{0,511},{1,2},{2,1},{3,4},{4,3},{5,6},{6,5},{7,8},{8,7},{9,10},{10... | collective-permute-start | bytes 3649544 | tf_op jit(solution)/shard_map/ppermute | solution.py:24
  28.3 3.3 %shard_map.69 = (f32[256,1152]{1,0:T(8,128)S(1)}, f32[256,1152]{1,0:T(8,128)S(1)}, f32[256,256]{1,0:T(8,128)S(1)}, f32[256,256]{1,0:T(8,128)S(1)}, bf16[256,1152...) custom-call(f32[1]{0:T(128)S(6)} %copy.27.scale, ...), custom_call_target="tpu_custom_call" | custom-call | bytes 8000000 | tf_op jit(solution)/shard_map/pallas_call | solution.py:272
  31.5 0.0 collective-permute-done.1.y1
  31.5 0.1 slice.6
  31.6 3.7 %collective-permute-start.2 = (f32[256,1152]{1,0:T(8,128)S(1)}, f32[256,1152]{1,0:T(8,128)S(1)}, u32[]{:S(2)}, u32[]{:S(2)}) collective-permute-start(f32[256,1152]{1,0:T(8,128)S(1)} %slice.6), channel_id=1, source_target_pairs={{0,1},{1,0},{2,3},{3,2},{4,5},{5,4},{6,7},{7,6},{8,9},{9,8},{10,11... | collective-permute-start | bytes 3538952 | tf_op jit(solution)/shard_map/ppermute | solution.py:29
  35.4 2.5 %collective-permute-done.2.y1s = f32[256,1152]{1,0:T(8,128)S(1)} collective-permute-done((f32[256,1152]{1,0:T(8,128)S(1)}, f32[256,1152]{1,0:T(8,128)S(1)}, u32[]{:S(2)}, u32[]{:S(2)}) %collective-permute-start.2) | collective-permute-done | bytes 1179680 | tf_op jit(solution)/shard_map/ppermute | solution.py:29
  37.8 1.6 %shard_map.70.after = f32[264,1152]{1,0:T(8,128)S(1)} custom-call(f32[1]{0:T(128)S(6)} %copy.27.scale, f32[1]{0:T(128)S(6)} %copy.28.shift, f32[264,1152]{1,0:T(8,128)S(1)} %collective-permute-done.1.y1, f32[256,1152]{1,0:T(8,128)S(1)} %collective-permute-done.2.y1s), custom_call_target="tpu_custom_call" | custom-call | tf_op jit(solution)/shard_map/pallas_call | solution.py:272
  39.4 2.2 %collective-permute-start.4 = (f32[264,1152]{1,0:T(8,128)S(1)}, f32[264,1152]{1,0:T(8,128)S(1)}, u32[]{:S(2)}, u32[]{:S(2)}) collective-permute-start(f32[264,1152]{1,0:T(8,128)S(1)} %shard_map.70.after), channel_id=1, source_target_pairs={{0,511},{1,2},{2,1},{3,4},{4,3},{5,6},{6,5},{7,8},{8,7},{9,10},{10... | collective-permute-start | bytes 3649544 | tf_op jit(solution)/shard_map/ppermute | solution.py:24
  41.6 3.0 %shard_map.71 = (f32[256,1152]{1,0:T(8,128)S(1)}, f32[256,1152]{1,0:T(8,128)S(1)}, f32[256,256]{1,0:T(8,128)S(1)}, f32[256,256]{1,0:T(8,128)S(1)}) custom-call(f32[1]{0:T(128)S(6)} %copy.27.scale, f32[1]{0:T(128)S(6)} %copy.28.shift, ...), custom_call_target="tpu_custom_call", output_to_operand_aliasing={{0}: (8, {}), {1}: (9, {}), {2}: (10, {}), {3}: (11, {})} | custom-call | tf_op jit(solution)/shard_map/pallas_call | solution.py:272
  44.6 0.0 collective-permute-done.3.y2
  44.6 0.1 slice.7
  44.6 6.2 %collective-permute-start.5 = (f32[256,1152]{1,0:T(8,128)S(1)}, f32[256,1152]{1,0:T(8,128)S(1)}, u32[]{:S(2)}, u32[]{:S(2)}) collective-permute-start(f32[256,1152]{1,0:T(8,128)S(1)} %slice.7), channel_id=1, source_target_pairs={{0,1},{1,0},{2,3},{3,2},{4,5},{5,4},{6,7},{7,6},{8,9},{9,8},{10,11... | collective-permute-start | bytes 3538952 | tf_op jit(solution)/shard_map/ppermute | solution.py:29
  50.9 1.9 %shard_map.72 = (f32[256,1152]{1,0:T(8,128)S(1)}, f32[256,1152]{1,0:T(8,128)S(1)}, f32[256,256]{1,0:T(8,128)S(1)}, f32[256,256]{1,0:T(8,128)S(1)}) custom-call(f32[1]{0:T(128)S(6)} %copy.27.scale, f32[1]{0:T(128)S(6)} %copy.28.shift, ...), custom_call_target="tpu_custom_call", output_to_operand_aliasing={{0}: (9, {}), {1}: (10, {}), {2}: (11, {}), {3}: (12, {})} | custom-call | tf_op jit(solution)/shard_map/pallas_call | solution.py:272
  52.7 0.6 %collective-permute-done.5.y2s = f32[256,1152]{1,0:T(8,128)S(1)} collective-permute-done((f32[256,1152]{1,0:T(8,128)S(1)}, f32[256,1152]{1,0:T(8,128)S(1)}, u32[]{:S(2)}, u32[]{:S(2)}) %collective-permute-start.5) | collective-permute-done | bytes 1179680 | tf_op jit(solution)/shard_map/ppermute | solution.py:29
  53.3 2.9 %shard_map.73 = (f32[256,1152]{1,0:T(8,128)}, f32[256,1152]{1,0:T(8,128)}, f32[8,256]{1,0:T(8,128)S(1)}, f32[8,256]{1,0:T(8,128)S(1)}) custom-call(f32[1]{0:T(128)S(6)} %copy.27.scale, f32[1]{0:T(128)S(6)} %copy.28.shift, bf16[256,1152]{1,0:T(8,128)(2,1)S(1)} %get-tuple-element.41.qh, bf16[256,1152]{1,0:T(8,128)(2,1)S(1)} %get-tuple-element.42.qlo, ...), custom_call_target="tpu_custom_call" | custom-call | tf_op jit(solution)/shard_map/pallas_call | solution.py:272
  56.3 1.3 %collective-permute-done.4.returned = f32[264,1152]{1,0:T(8,128)S(1)} collective-permute-done((f32[264,1152]{1,0:T(8,128)S(1)}, f32[264,1152]{1,0:T(8,128)S(1)}, u32[]{:S(2)}, u32[]{:S(2)}) %collective-permute-start.4) | collective-permute-done | bytes 1216544 | tf_op jit(solution)/shard_map/ppermute | solution.py:24
  57.6 1.4 %shard_map.74 = (f32[1,256]{1,0:T(1,128)}, f32[256,1152]{1,0:T(8,128)}, f32[256,1152]{1,0:T(8,128)}) custom-call(f32[256,1152]{1,0:T(8,128)S(1)} %get-tuple-element.58.gp_in, f32[264,1152]{1,0:T(8,128)S(1)} %collective-permute-done.4.returned, f32[264,1152]{1,0:T(8,128)S(1)} %get-tuple-element.37.p, ...), custom_call_target="tpu_custom_call", output_to_operand_aliasing={{1}: (6, {}), {2}: (7, {})} | custom-call | tf_op jit(solution)/shard_map/pallas_call | solution.py:272
Async XLA Ops:
  2.1 29.4 %collective-permute-start.1 = (f32[264,1152]{1,0:T(8,128)S(1)}, f32[264,1152]{1,0:T(8,128)S(1)}, u32[]{:S(2)}, u32[]{:S(2)}) collective-permute-start(f32[264,1152]{1,0:T(8,128)S(1)} %get-tuple-element.37.p), channel_id=1, source_target_pairs={{0,511},{1,2},{2,1},{3,4},{4,3},{5,6},{6,5},{7,8},{8,7},{9,10},{10... | collective-permute-start | bytes 3649544 | tf_op jit(solution)/shard_map/ppermute | solution.py:24
  8.1 16.9 %collective-permute-start = (f32[256,1152]{1,0:T(8,128)S(1)}, f32[256,1152]{1,0:T(8,128)S(1)}, u32[]{:S(2)}, u32[]{:S(2)}) collective-permute-start(f32[256,1152]{1,0:T(8,128)S(1)} %get-tuple-element.38.q), channel_id=1, source_target_pairs={{0,1},{1,0},{2,3},{3,2},{4,5},{5,4},{6,7},{7,6},{8,9},{9,8},{10,11... | collective-permute-start | bytes 3538952 | tf_op jit(solution)/shard_map/ppermute | solution.py:29
  25.0 19.5 %collective-permute-start.3 = (f32[264,1152]{1,0:T(8,128)S(1)}, f32[264,1152]{1,0:T(8,128)S(1)}, u32[]{:S(2)}, u32[]{:S(2)}) collective-permute-start(f32[264,1152]{1,0:T(8,128)S(1)} %pad.4), channel_id=1, source_target_pairs={{0,511},{1,2},{2,1},{3,4},{4,3},{5,6},{6,5},{7,8},{8,7},{9,10},{10... | collective-permute-start | bytes 3649544 | tf_op jit(solution)/shard_map/ppermute | solution.py:24
  31.6 6.2 %collective-permute-start.2 = (f32[256,1152]{1,0:T(8,128)S(1)}, f32[256,1152]{1,0:T(8,128)S(1)}, u32[]{:S(2)}, u32[]{:S(2)}) collective-permute-start(f32[256,1152]{1,0:T(8,128)S(1)} %slice.6), channel_id=1, source_target_pairs={{0,1},{1,0},{2,3},{3,2},{4,5},{5,4},{6,7},{7,6},{8,9},{9,8},{10,11... | collective-permute-start | bytes 3538952 | tf_op jit(solution)/shard_map/ppermute | solution.py:29
  39.4 18.2 %collective-permute-start.4 = (f32[264,1152]{1,0:T(8,128)S(1)}, f32[264,1152]{1,0:T(8,128)S(1)}, u32[]{:S(2)}, u32[]{:S(2)}) collective-permute-start(f32[264,1152]{1,0:T(8,128)S(1)} %shard_map.70.after), channel_id=1, source_target_pairs={{0,511},{1,2},{2,1},{3,4},{4,3},{5,6},{6,5},{7,8},{8,7},{9,10},{10... | collective-permute-start | bytes 3649544 | tf_op jit(solution)/shard_map/ppermute | solution.py:24
  44.6 8.7 %collective-permute-start.5 = (f32[256,1152]{1,0:T(8,128)S(1)}, f32[256,1152]{1,0:T(8,128)S(1)}, u32[]{:S(2)}, u32[]{:S(2)}) collective-permute-start(f32[256,1152]{1,0:T(8,128)S(1)} %slice.7), channel_id=1, source_target_pairs={{0,1},{1,0},{2,3},{3,2},{4,5},{5,4},{6,7},{7,6},{8,9},{9,8},{10,11... | collective-permute-start | bytes 3538952 | tf_op jit(solution)/shard_map/ppermute | solution.py:29

commit v6 on v5

--- a/solution.py
+++ b/solution.py
@@ -15,7 +15,8 @@
 PAD = 8
 COST_Q = 8000000
 COST_OWN = 8000000
-VMEM_LIMIT = 24 * 1024 * 1024
+COST_SPLIT = 4000000
+VMEM_LIMIT = 20 * 1024 * 1024
 
 
 def across(value):
@@ -27,6 +28,11 @@
 def in_chip(value):
     count = lax.axis_size("blk")
     return lax.ppermute(value, "blk", [(i, i ^ 1) for i in range(count)])
+
+
+def in_chip_in_halves(value):
+    half = value.shape[0] // 2
+    return jnp.concatenate([in_chip(value[:half]), in_chip(value[half:])], axis=0)
 
 
 def split(value):
@@ -72,7 +78,11 @@
     return jnp.transpose(jnp.broadcast_to(sums, (terms.shape[0], 128)))[:8]
 
 
-def pick_kernel(odd_takes, image, text, unit, inverse, raw, sem):
+def inverse_norm(value):
+    return lax.rsqrt(jnp.sum(value * value, axis=1, keepdims=True) + EPS)
+
+
+def pick_kernel(odd_takes, image, text, unit, raw, sem):
     rows = raw.shape[0] // CHUNKS
     takes_image = lax.rem(lax.axis_index("blk"), 2) != odd_takes
 
@@ -97,18 +107,22 @@
         copy(image, c).wait()
         part = pl.ds(c * rows, rows)
         value = raw[part]
-        inv = lax.rsqrt(jnp.sum(value * value, axis=1, keepdims=True) + EPS)
-        unit[part] = value * inv
-        inverse[part] = jnp.broadcast_to(inv, (rows, 128))
-
-
-def middle_kernel(scale, shift, y1, y1s, sent, tile, yh, yl, sh, sl):
+        unit[part] = value * inverse_norm(value)
+
+
+def split_kernel(value, high, low, raw, sem):
+    read = pltpu.make_async_copy(value, raw, sem)
+    read.start()
+    read.wait()
+    high[...], low[...] = split(raw[...])
+
+
+def middle_kernel(scale, shift, yh, yl, y1s, sent, tile, sh, sl):
     rows, width = yh.shape
 
     @step(0)
     def _():
         sh[...], sl[...] = split(y1s[...])
-        yh[...], yl[...] = split(y1[: yh.shape[0]])
         tile[...] = logits((yh[...], yl[...]), (sh[...], sl[...]))
 
     @step(1)
@@ -119,63 +133,73 @@
         sent[rows:, rows:] = jnp.zeros((8, width - rows), F32)
 
 
-def own_kernel(
-    scale, shift, p, q, z, grad_p, grad_q, loss_p, loss_q, ph, plo, qh, qlo, zh, zl, tile_own, tile_z
+def own_kernel(scale, shift, p, q, grad_p, grad_q, loss_p, loss_q, ph, plo, qh, qlo, tile):
+    rows = ph.shape[0]
+
+    @step(0)
+    def _():
+        ph[...], plo[...] = split(p[...])
+        qh[...], qlo[...] = split(q[:rows])
+        tile[...] = logits((ph[...], plo[...]), (qh[...], qlo[...]))
+
+    @step(1)
+    def _():
+        terms, weight = pair_terms(tile[...], scale[0], shift[0], own=True)
+        loss_p[...] = terms
+        loss_q[...] = jnp.transpose(terms)
+        grad_p[...] = spread(weight, (qh[...], qlo[...]))
+        grad_q[...] = spread(jnp.transpose(weight), (ph[...], plo[...]))
+
+
+def add_first(
+    scale, shift, ph, plo, qh, qlo, yh, yl, y1s, z, gp_in, gq_in, lp_in, lq_in, grad_p, grad_q, loss_p, loss_q, scratch
 ):
-    @step(0)
-    def _():
-        ph[...], plo[...] = split(p[: ph.shape[0]])
-        qh[...], qlo[...] = split(q[...])
-        tile_own[...] = logits((ph[...], plo[...]), (qh[...], qlo[...]))
-        zh[...], zl[...] = split(z[...])
-        tile_z[...] = logits((qh[...], qlo[...]), (zh[...], zl[...]))
-
-    @step(1)
-    def _():
-        terms, weight = pair_terms(tile_own[...], scale[0], shift[0], own=True)
-        terms_z, weight_z = pair_terms(tile_z[...], scale[0], shift[0])
-        loss_p[...] = terms
-        loss_q[...] = jnp.transpose(terms) + terms_z
-        grad_p[...] = spread(weight, (qh[...], qlo[...]))
-        grad_q[...] = spread(jnp.transpose(weight), (ph[...], plo[...])) + spread(weight_z, (zh[...], zl[...]))
-
-
-def add_first(scale, shift, ph, plo, qh, qlo, y1, y1s, gp_in, gq_in, lp_in, lq_in, grad_p, grad_q, loss_p, loss_q, scratch):
-    yh, yl, sh, sl, tile_y, tile_s = scratch
+    sh, sl, zh, zl, tile_y, tile_s, tile_z, z_raw, sem = scratch
+    rows = ph.shape[0]
+    read = pltpu.make_async_copy(z.at[pl.ds(0, rows)], z_raw, sem)
 
     def logit_part():
-        yh[...], yl[...] = split(y1[: yh.shape[0]])
+        read.start()
         tile_y[...] = logits((ph[...], plo[...]), (yh[...], yl[...]))
         sh[...], sl[...] = split(y1s[...])
         tile_s[...] = logits((qh[...], qlo[...]), (sh[...], sl[...]))
 
+    def partner_part():
+        read.wait()
+        zh[...], zl[...] = split(z_raw[...])
+        tile_z[...] = logits((qh[...], qlo[...]), (zh[...], zl[...]))
+
     def gradient_part():
         terms_y, weight_y = pair_terms(tile_y[...], scale[0], shift[0])
         terms_s, weight_s = pair_terms(tile_s[...], scale[0], shift[0])
+        terms_z, weight_z = pair_terms(tile_z[...], scale[0], shift[0])
         loss_p[...] = lp_in[...] + terms_y
-        loss_q[...] = lq_in[...] + terms_s
+        loss_q[...] = lq_in[...] + terms_s + terms_z
         grad_p[...] = gp_in[...] + spread(weight_y, (yh[...], yl[...]))
-        grad_q[...] = gq_in[...] + spread(weight_s, (sh[...], sl[...]))
-
-    return logit_part, gradient_part
+        grad_q[...] = gq_in[...] + spread(weight_s, (sh[...], sl[...])) + spread(weight_z, (zh[...], zl[...]))
+
+    return logit_part, partner_part, gradient_part
 
 
 def odd_first_kernel(
-    scale, shift, ph, plo, qh, qlo, y1, y1s, gp_in, gq_in, lp_in, lq_in, after, grad_p, grad_q, loss_p, loss_q, *scratch
+    scale, shift, ph, plo, qh, qlo, yh, yl, y1s, z, gp_in, gq_in, lp_in, lq_in, after, grad_p, grad_q, loss_p, loss_q, *scratch
 ):
     parts = add_first(
-        scale, shift, ph, plo, qh, qlo, y1, y1s, gp_in, gq_in, lp_in, lq_in, grad_p, grad_q, loss_p, loss_q, scratch
+        scale, shift, ph, plo, qh, qlo, yh, yl, y1s, z, gp_in, gq_in, lp_in, lq_in, grad_p, grad_q, loss_p, loss_q, scratch
     )
     for part in parts:
         pl.when(lax.rem(lax.axis_index("blk"), 2) == 1)(part)
 
 
 def even_first_kernel(
-    scale, shift, ph, plo, qh, qlo, y1, y1s, y2, gp_in, gq_in, lp_in, lq_in, grad_p, grad_q, loss_p, loss_q,
-    wh, wl, tile_w, *scratch
+    scale, shift, ph, plo, qh, qlo, yh, yl, y1s, z, y2, image, text, gp_in, gq_in, lp_in, lq_in,
+    grad_p, grad_q, loss_p, loss_q, inv_p, inv_q, wh, wl, tile_w, raw, raw_sem, *scratch
 ):
+    reads = [pltpu.make_async_copy(side, raw.at[i], raw_sem.at[i]) for i, side in enumerate((image, text))]
+    for read in reads:
+        read.start()
     parts = add_first(
-        scale, shift, ph, plo, qh, qlo, y1, y1s, gp_in, gq_in, lp_in, lq_in, grad_p, grad_q, loss_p, loss_q, scratch
+        scale, shift, ph, plo, qh, qlo, yh, yl, y1s, z, gp_in, gq_in, lp_in, lq_in, grad_p, grad_q, loss_p, loss_q, scratch
     )
     for part in parts:
         pl.when(lax.rem(lax.axis_index("blk"), 2) == 0)(part)
@@ -190,6 +214,12 @@
         terms, weight = pair_terms(tile_w[...], scale[0], shift[0])
         loss_p[...] = lp_in[...] + terms
         grad_p[...] = gp_in[...] + spread(weight, (wh[...], wl[...]))
+
+    for read in reads:
+        read.wait()
+    odd = lax.rem(lax.axis_index("blk"), 2)
+    inv_p[...] = jnp.broadcast_to(inverse_norm(raw[odd]), inv_p.shape)
+    inv_q[...] = jnp.broadcast_to(inverse_norm(raw[1 - odd]), inv_q.shape)
 
 
 def restored(unit, inverse, grad):
@@ -298,52 +328,59 @@
         return call(
             functools.partial(pick_kernel, odd_takes),
             [(picture_vectors, hbm), (caption_vectors, hbm)],
-            [fast((taken, width)), fast((rows, 128))],
+            [fast((taken, width))],
             [pltpu.VMEM(block, F32), pltpu.SemaphoreType.DMA((CHUNKS,))],
             cost=cost,
         )
 
     line, square, half = (8, rows), (rows, rows), pltpu.VMEM(block, BF16)
     tile = pltpu.VMEM(square, F32)
-    p, inv_p = pick(1, rows + PAD, 0)
+    (p,) = pick(1, rows, 0)
     y1 = across(p)
-    q, inv_q = pick(0, rows, COST_Q)
-    z = in_chip(q)
-    y2 = across(jnp.pad(z, ((0, PAD), (0, 0))))
+    (q,) = pick(0, rows + PAD, COST_Q)
+    z = lax.cond(lax.axis_index("blk") < 1 << 20, in_chip, in_chip_in_halves, q)
+    y2 = across(z)
     grad_p, grad_q, loss_p, loss_q, ph, plo, qh, qlo = call(
         own_kernel,
-        scalars + v(p, q, z),
+        scalars + v(p, q),
         [fast(), fast(), fast(square), fast(square)] + [fast(block, BF16)] * 4,
-        [half] * 2 + [tile] * 2,
+        [tile],
         cost=COST_OWN,
     )
     y1, grad_p = lax.optimization_barrier((y1, grad_p))
-    y1s = in_chip(y1[:rows])
+    y1s = in_chip(y1)
+    yh, yl = call(
+        split_kernel,
+        [(y1, hbm)],
+        [fast(block, BF16)] * 2,
+        [pltpu.VMEM(block, F32), pltpu.SemaphoreType.DMA],
+        cost=COST_SPLIT,
+    )
     (sent,) = call(
         middle_kernel,
-        scalars + v(y1, y1s),
+        scalars + v(yh, yl, y1s),
         [fast((rows + 8, width))],
-        [tile] + [half] * 4,
+        [tile] + [half] * 2,
     )
     returned = across(sent)
     state = [grad_p, grad_q, loss_p, loss_q]
     outs = [fast(), fast(), fast(square), fast(square)]
-    scratch = [half] * 4 + [tile] * 2
+    scratch = [half] * 4 + [tile] * 3 + [pltpu.VMEM(block, F32), pltpu.SemaphoreType.DMA]
     state = call(
         odd_first_kernel,
-        scalars + v(ph, plo, qh, qlo, y1, y1s, *state) + [(sent, anywhere)],
+        scalars + v(ph, plo, qh, qlo, yh, yl, y1s) + [(z, hbm)] + v(*state) + [(sent, anywhere)],
         outs,
         scratch,
-        {8 + i: i for i in range(4)},
+        {10 + i: i for i in range(4)},
     )
     y2, state = lax.optimization_barrier((y2, state))
     y2s = in_chip(y2[:rows])
-    grad_p, grad_q, loss_p, loss_q = call(
+    grad_p, grad_q, loss_p, loss_q, inv_p, inv_q = call(
         even_first_kernel,
-        scalars + v(ph, plo, qh, qlo, y1, y1s, y2, *state),
-        outs,
-        [half, half, tile] + scratch,
-        {9 + i: i for i in range(4)},
+        scalars + v(ph, plo, qh, qlo, yh, yl, y1s) + [(z, hbm)] + v(y2) + [(picture_vectors, hbm), (caption_vectors, hbm)] + v(*state),
+        outs + [fast((rows, 128))] * 2,
+        [half, half, tile, pltpu.VMEM((2, rows, width), F32), pltpu.SemaphoreType.DMA((2,))] + scratch,
+        {13 + i: i for i in range(4)},
     )
     whole = (jax.ShapeDtypeStruct(block, F32), hbm)
     out_scratch = [pltpu.VMEM(block, F32), pltpu.SemaphoreType.DMA((CHUNKS,))]

time: 59.5 us -> 59.3 us (level)
  waiting for transfers between devices: 6.83 us -> 5.08 us
  Pallas kernels: 16.9 us -> 18.5 us
    pallas_call x8 -> x9, Pallas kernels: 16.9 us -> 18.5 us  [call(): pl.pallas_call(kernel, out_shape=[o for o, _ in outs], in_specs=specs, ou...]
    ppermute x3, waiting for transfers between devices: 5.5 us -> 4.13 us  [in_chip(): return lax.ppermute(value, 'blk', [(i, i ^ 1) for i in range(count)])]
  transfers between devices with their start and end apart: 6 -> 6, of which waited for: 4 -> 4; matrix products, arithmetic and copies ran while one was open for 0% -> 0% of each run, Pallas kernels for 24% -> 27%
where the time goes in v6:
time: 59.3 us; the launch traced here: 58.9 us
  starting transfers between devices  33 us (56%)
  Pallas kernels  18.5 us (31%)
  waiting for transfers between devices  5.08 us (9%)
  between operations  2.21 us (4%)
    ppermute x3, starting transfers between devices, in_chip(): return lax.ppermute(value, 'blk', [(i, i ^ 1) for i in range(count)])  24.6 us
    pallas_call x9, Pallas kernels, call(): pl.pallas_call(kernel, out_shape=[o for o, _ in outs], in_specs=specs, ou...  18.5 us
    ppermute x3, starting transfers between devices, across(): return lax.ppermute(value, 'blk', pairs)  8.34 us
    ppermute x3, waiting for transfers between devices, in_chip(): return lax.ppermute(value, 'blk', [(i, i ^ 1) for i in range(count)])  4.13 us
  transfers between devices with their start and end apart: 6, of which 4 were waited for; matrix products, arithmetic and copies ran while one was open for 0% of the time, Pallas kernels for 27%

profile of v6, /device:TPU:1, one launch (start us, length us, event | category | flops | bytes accessed | tf_op | source)
XLA Modules:
  0.0 58.9 jit_solution(1285251598147732528)
XLA Ops:
  0.6 1.5 %shard_map.67.p = f32[256,1152]{1,0:T(8,128)S(1)} custom-call(f32[256,1152]{1,0:T(8,128)} %image.5, f32[256,1152]{1,0:T(8,128)} %text.5), custom_call_target="tpu_custom_call" | custom-call | tf_op jit(solution)/shard_map/pallas_call | solution.py:302
  2.1 4.5 %collective-permute-start.3 = (f32[256,1152]{1,0:T(8,128)S(1)}, f32[256,1152]{1,0:T(8,128)}, u32[]{:S(2)}, u32[]{:S(2)}) collective-permute-start(f32[256,1152]{1,0:T(8,128)S(1)} %shard_map.67.p), channel_id=1, source_target_pairs={{0,511},{1,2},{2,1},{3,4},{4,3},{5,6},{6,5},{7,8},{8,7},{9,10},{10... | collective-permute-start | bytes 3538952 | tf_op jit(solution)/shard_map/ppermute | solution.py:25
  6.6 1.5 %shard_map.68.q = f32[264,1152]{1,0:T(8,128)S(1)} custom-call(f32[256,1152]{1,0:T(8,128)} %image.5, f32[256,1152]{1,0:T(8,128)} %text.5), custom_call_target="tpu_custom_call" | custom-call | bytes 8000000 | tf_op jit(solution)/shard_map/pallas_call | solution.py:302
  8.1 17.0 %conditional.1 = (f32[264,1152]{1,0:T(8,128)}) conditional(s32[]{:T(128)} %convert_element_type.3, f32[264,1152]{1,0:T(8,128)S(1)} %shard_map.68.q, f32[264,1152]{1,0:T(8,128)S(1)} %shard_map.68.q), branch_computations={%region_0.0_spmd, %region_1.0_spmd} | conditional | bytes 9732184 | solution.py:341
  8.1 14.4 %collective-permute-start = (f32[264,1152]{1,0:T(8,128)S(1)}, f32[264,1152]{1,0:T(8,128)}, u32[]{:S(2)}, u32[]{:S(2)}) collective-permute-start(f32[264,1152]{1,0:T(8,128)S(1)} %param.1), channel_id=1, source_target_pairs={{0,1},{1,0},{2,3},{3,2},{4,5},{5,4},{6,7},{7,6},{8,9},{9,8},{10,11... | collective-permute-start | bytes 3649544 | tf_op jit(solution)/shard_map/cond/branch_1_fun/ppermute | solution.py:30
  22.5 2.6 %collective-permute-done = f32[264,1152]{1,0:T(8,128)} collective-permute-done((f32[264,1152]{1,0:T(8,128)S(1)}, f32[264,1152]{1,0:T(8,128)}, u32[]{:S(2)}, u32[]{:S(2)}) %collective-permute-start) | collective-permute-done | bytes 1216544 | tf_op jit(solution)/shard_map/cond/branch_1_fun/ppermute | solution.py:30
  25.1 1.9 %collective-permute-start.5 = (f32[264,1152]{1,0:T(8,128)}, f32[264,1152]{1,0:T(8,128)S(1)}, u32[]{:S(2)}, u32[]{:S(2)}) collective-permute-start(f32[264,1152]{1,0:T(8,128)} %get-tuple-element.78.z), channel_id=1, source_target_pairs={{0,511},{1,2},{2,1},{3,4},{4,3},{5,6},{6,5},{7,8},{8,7},{9,10},{10... | collective-permute-start | bytes 3649544 | tf_op jit(solution)/shard_map/ppermute | solution.py:25
  28.3 2.1 %shard_map.69 = (f32[256,1152]{1,0:T(8,128)S(1)}, f32[256,1152]{1,0:T(8,128)S(1)}, f32[256,256]{1,0:T(8,128)S(1)}, f32[256,256]{1,0:T(8,128)S(1)}, bf16[256,1152...) custom-call(f32[1]{0:T(128)S(6)} %copy.29.scale, ...), custom_call_target="tpu_custom_call" | custom-call | bytes 8000000 | tf_op jit(solution)/shard_map/pallas_call | solution.py:302
  30.5 0.0 collective-permute-done.3.value
  30.5 4.5 %collective-permute-start.4 = (f32[256,1152]{1,0:T(8,128)}, f32[256,1152]{1,0:T(8,128)S(1)}, u32[]{:S(2)}, u32[]{:S(2)}) collective-permute-start(f32[256,1152]{1,0:T(8,128)} %collective-permute-done.3.value), channel_id=1, source_target_pairs={{0,1},{1,0},{2,3},{3,2},{4,5},{5,4},{6,7},{7,6},{8,9},{9,8},{10,11... | collective-permute-start | bytes 3538952 | tf_op jit(solution)/shard_map/ppermute | solution.py:30
  35.0 1.4 %shard_map.70 = (bf16[256,1152]{1,0:T(8,128)(2,1)S(1)}, bf16[256,1152]{1,0:T(8,128)(2,1)S(1)}) custom-call(f32[256,1152]{1,0:T(8,128)} %collective-permute-done.3.value), custom_call_target="tpu_custom_call" | custom-call | bytes 4000000 | tf_op jit(solution)/shard_map/pallas_call | solution.py:302
  36.4 1.2 %collective-permute-done.4.y1s = f32[256,1152]{1,0:T(8,128)S(1)} collective-permute-done((f32[256,1152]{1,0:T(8,128)}, f32[256,1152]{1,0:T(8,128)S(1)}, u32[]{:S(2)}, u32[]{:S(2)}) %collective-permute-start.4) | collective-permute-done | bytes 1179680 | tf_op jit(solution)/shard_map/ppermute | solution.py:30
  37.6 1.5 %shard_map.71.after = f32[264,1152]{1,0:T(8,128)S(1)} custom-call(f32[1]{0:T(128)S(6)} %copy.29.scale, f32[1]{0:T(128)S(6)} %copy.30.shift, bf16[256,1152]{1,0:T(8,128)(2,1)S(1)} %get-tuple-element.48.yh, bf16[256,1152]{1,0:T(8,128)(2,1)S(1)} %get-tuple-element.49.yl, f32[256,1152]{1,0:T(8,128)S(1)} %collective-permute-done.4.y1s), custom_call_target="tpu_custom_call" | custom-call | tf_op jit(solution)/shard_map/pallas_call | solution.py:302
  39.1 1.9 %collective-permute-start.6 = (f32[264,1152]{1,0:T(8,128)S(1)}, f32[264,1152]{1,0:T(8,128)S(1)}, u32[]{:S(2)}, u32[]{:S(2)}) collective-permute-start(f32[264,1152]{1,0:T(8,128)S(1)} %shard_map.71.after), channel_id=1, source_target_pairs={{0,511},{1,2},{2,1},{3,4},{4,3},{5,6},{6,5},{7,8},{8,7},{9,10},{10... | collective-permute-start | bytes 3649544 | tf_op jit(solution)/shard_map/ppermute | solution.py:25
  41.1 4.1 %shard_map.72 = (f32[256,1152]{1,0:T(8,128)S(1)}, f32[256,1152]{1,0:T(8,128)S(1)}, f32[256,256]{1,0:T(8,128)S(1)}, f32[256,256]{1,0:T(8,128)S(1)}) custom-call(f32[1]{0:T(128)S(6)} %copy.29.scale, f32[1]{0:T(128)S(6)} %copy.30.shift, ...), custom_call_target="tpu_custom_call", output_to_operand_aliasing={{0}: (10, {}), {1}: (11, {}), {2}: (12, {}), {3}: (13, {})} | custom-call | tf_op jit(solution)/shard_map/pallas_call | solution.py:302
  45.2 0.0 collective-permute-done.5.y2
  45.2 0.1 slice.9
  45.3 5.7 %collective-permute-start.7 = (f32[256,1152]{1,0:T(8,128)S(1)}, f32[256,1152]{1,0:T(8,128)S(1)}, u32[]{:S(2)}, u32[]{:S(2)}) collective-permute-start(f32[256,1152]{1,0:T(8,128)S(1)} %slice.9), channel_id=1, source_target_pairs={{0,1},{1,0},{2,3},{3,2},{4,5},{5,4},{6,7},{7,6},{8,9},{9,8},{10,11... | collective-permute-start | bytes 3538952 | tf_op jit(solution)/shard_map/ppermute | solution.py:30
  51.0 2.2 %shard_map.73 = (f32[256,1152]{1,0:T(8,128)S(1)}, f32[256,1152]{1,0:T(8,128)S(1)}, f32[256,256]{1,0:T(8,128)S(1)}, f32[256,256]{1,0:T(8,128)S(1)}, f32[256,128]{1,0:T(8,128)S(1)}, /*index=5*/f32[256,128]{1,0:T(8,128)S(1)}) custom-call(f32[1]{0:T(128)S(6)} %copy.29.scale, ...), custom_call_target="tpu_custom_call", output_to_operand_aliasing={{0}: (13, {}), {1}: (14, {}), {2}: (15, {}), {3}: (16, {})} | custom-call | tf_op jit(solution)/shard_map/pallas_call | solution.py:302
  53.2 0.3 collective-permute-done.7.y2s
  53.5 2.9 %shard_map.74 = (f32[256,1152]{1,0:T(8,128)}, f32[256,1152]{1,0:T(8,128)}, f32[8,256]{1,0:T(8,128)S(1)}, f32[8,256]{1,0:T(8,128)S(1)}) custom-call(f32[1]{0:T(128)S(6)} %copy.29.scale, f32[1]{0:T(128)S(6)} %copy.30.shift, bf16[256,1152]{1,0:T(8,128)(2,1)S(1)} %get-tuple-element.44.qh, bf16[256,1152]{1,0:T(8,128)(2,1)S(1)} %get-tuple-element.45.qlo, ...), custom_call_target="tpu_custom_call" | custom-call | tf_op jit(solution)/shard_map/pallas_call | solution.py:302
  56.4 0.9 %collective-permute-done.6.returned = f32[264,1152]{1,0:T(8,128)S(1)} collective-permute-done((f32[264,1152]{1,0:T(8,128)S(1)}, f32[264,1152]{1,0:T(8,128)S(1)}, u32[]{:S(2)}, u32[]{:S(2)}) %collective-permute-start.6) | collective-permute-done | bytes 1216544 | tf_op jit(solution)/shard_map/ppermute | solution.py:25
  57.3 1.4 %shard_map.75 = (f32[1,256]{1,0:T(1,128)}, f32[256,1152]{1,0:T(8,128)}, f32[256,1152]{1,0:T(8,128)}) custom-call(f32[256,1152]{1,0:T(8,128)S(1)} %get-tuple-element.63.gp_in, f32[264,1152]{1,0:T(8,128)S(1)} %collective-permute-done.6.returned, f32[256,1152]{1,0:T(8,128)S(1)} %shard_map.67.p, ...), custom_call_target="tpu_custom_call", output_to_operand_aliasing={{1}: (6, {}), {2}: (7, {})} | custom-call | tf_op jit(solution)/shard_map/pallas_call | solution.py:302
Async XLA Ops:
  2.1 28.4 %collective-permute-start.3 = (f32[256,1152]{1,0:T(8,128)S(1)}, f32[256,1152]{1,0:T(8,128)}, u32[]{:S(2)}, u32[]{:S(2)}) collective-permute-start(f32[256,1152]{1,0:T(8,128)S(1)} %shard_map.67.p), channel_id=1, source_target_pairs={{0,511},{1,2},{2,1},{3,4},{4,3},{5,6},{6,5},{7,8},{8,7},{9,10},{10... | collective-permute-start | bytes 3538952 | tf_op jit(solution)/shard_map/ppermute | solution.py:25
  8.1 17.0 %collective-permute-start = (f32[264,1152]{1,0:T(8,128)S(1)}, f32[264,1152]{1,0:T(8,128)}, u32[]{:S(2)}, u32[]{:S(2)}) collective-permute-start(f32[264,1152]{1,0:T(8,128)S(1)} %param.1), channel_id=1, source_target_pairs={{0,1},{1,0},{2,3},{3,2},{4,5},{5,4},{6,7},{7,6},{8,9},{9,8},{10,11... | collective-permute-start | bytes 3649544 | tf_op jit(solution)/shard_map/cond/branch_1_fun/ppermute | solution.py:30
  25.1 20.1 %collective-permute-start.5 = (f32[264,1152]{1,0:T(8,128)}, f32[264,1152]{1,0:T(8,128)S(1)}, u32[]{:S(2)}, u32[]{:S(2)}) collective-permute-start(f32[264,1152]{1,0:T(8,128)} %get-tuple-element.78.z), channel_id=1, source_target_pairs={{0,511},{1,2},{2,1},{3,4},{4,3},{5,6},{6,5},{7,8},{8,7},{9,10},{10... | collective-permute-start | bytes 3649544 | tf_op jit(solution)/shard_map/ppermute | solution.py:25
  30.5 7.2 %collective-permute-start.4 = (f32[256,1152]{1,0:T(8,128)}, f32[256,1152]{1,0:T(8,128)S(1)}, u32[]{:S(2)}, u32[]{:S(2)}) collective-permute-start(f32[256,1152]{1,0:T(8,128)} %collective-permute-done.3.value), channel_id=1, source_target_pairs={{0,1},{1,0},{2,3},{3,2},{4,5},{5,4},{6,7},{7,6},{8,9},{9,8},{10,11... | collective-permute-start | bytes 3538952 | tf_op jit(solution)/shard_map/ppermute | solution.py:30
  39.1 18.2 %collective-permute-start.6 = (f32[264,1152]{1,0:T(8,128)S(1)}, f32[264,1152]{1,0:T(8,128)S(1)}, u32[]{:S(2)}, u32[]{:S(2)}) collective-permute-start(f32[264,1152]{1,0:T(8,128)S(1)} %shard_map.71.after), channel_id=1, source_target_pairs={{0,511},{1,2},{2,1},{3,4},{4,3},{5,6},{6,5},{7,8},{8,7},{9,10},{10... | collective-permute-start | bytes 3649544 | tf_op jit(solution)/shard_map/ppermute | solution.py:25
  45.3 8.2 %collective-permute-start.7 = (f32[256,1152]{1,0:T(8,128)S(1)}, f32[256,1152]{1,0:T(8,128)S(1)}, u32[]{:S(2)}, u32[]{:S(2)}) collective-permute-start(f32[256,1152]{1,0:T(8,128)S(1)} %slice.9), channel_id=1, source_target_pairs={{0,1},{1,0},{2,3},{3,2},{4,5},{5,4},{6,7},{7,6},{8,9},{9,8},{10,11... | collective-permute-start | bytes 3538952 | tf_op jit(solution)/shard_map/ppermute | solution.py:30

commit v7 on v6

--- a/solution.py
+++ b/solution.py
@@ -11,7 +11,8 @@
 EPS = 1e-06
 F32 = jnp.float32
 BF16 = jnp.bfloat16
-CHUNKS = 4
+READ_ROWS = (64, 64, 64, 64)
+WRITE_ROWS = (16, 64, 80, 96)
 PAD = 8
 COST_Q = 8000000
 COST_OWN = 8000000
@@ -82,30 +83,35 @@
     return lax.rsqrt(jnp.sum(value * value, axis=1, keepdims=True) + EPS)
 
 
+def parts_of(rows):
+    starts = [sum(rows[:i]) for i in range(len(rows))]
+    return [pl.ds(start, size) for start, size in zip(starts, rows)]
+
+
 def pick_kernel(odd_takes, image, text, unit, raw, sem):
-    rows = raw.shape[0] // CHUNKS
+    parts = parts_of(READ_ROWS)
     takes_image = lax.rem(lax.axis_index("blk"), 2) != odd_takes
 
     def copy(source, c):
-        part = pl.ds(c * rows, rows)
+        part = parts[c]
         return pltpu.make_async_copy(source.at[part], raw.at[part], sem.at[c])
 
     @pl.when(takes_image)
     def _():
-        for c in range(CHUNKS):
+        for c in range(len(parts)):
             copy(image, c).start()
 
     @pl.when(jnp.logical_not(takes_image))
     def _():
-        for c in range(CHUNKS):
+        for c in range(len(parts)):
             copy(text, c).start()
 
     extra = unit.shape[0] - raw.shape[0]
     if extra:
         unit[raw.shape[0] :] = jnp.zeros((extra, raw.shape[1]), F32)
-    for c in range(CHUNKS):
+    for c in range(len(parts)):
         copy(image, c).wait()
-        part = pl.ds(c * rows, rows)
+        part = parts[c]
         value = raw[part]
         unit[part] = value * inverse_norm(value)
 
@@ -227,9 +233,7 @@
     return inverse * (grad - inner * unit)
 
 
-def put(value_ref, image_out, text_out, to_image, sem, c, rows):
-    part = pl.ds(c * rows, rows)
-
+def put(value_ref, image_out, text_out, to_image, sem, c, part):
     @pl.when(to_image)
     def _():
         pltpu.make_async_copy(value_ref.at[part], image_out.at[part], sem.at[c]).start()
@@ -240,13 +244,11 @@
 
 
 def finish(unit, inverse, grad, image_out, text_out, result, sem, to_image):
-    rows = result.shape[0] // CHUNKS
-    for c in range(CHUNKS):
-        part = pl.ds(c * rows, rows)
+    parts = parts_of(WRITE_ROWS)
+    for c, part in enumerate(parts):
         result[part] = restored(unit[part], inverse[part][:, :1], grad(part))
-        put(result, image_out, text_out, to_image, sem, c, rows)
-    for c in range(CHUNKS):
-        part = pl.ds(c * rows, rows)
+        put(result, image_out, text_out, to_image, sem, c, part)
+    for c, part in enumerate(parts):
         pltpu.make_async_copy(result.at[part], image_out.at[part], sem.at[c]).wait()
 
 
@@ -270,7 +272,7 @@
             grad = gq_in[part] + spread(weight, (sh[...], sl[...]))
             result[part] = restored(q[part], inv_q[part][:, :1], grad)
             tile_s[part] = lq_in[part] + terms
-            put(result, image_out, text_out, odd, sem, h, rows)
+            put(result, image_out, text_out, odd, sem, h, part)
 
     loss_q[...] = row_sums(tile_s[...])
     loss_p[...] = row_sums(lp_in[...])
@@ -329,7 +331,7 @@
             functools.partial(pick_kernel, odd_takes),
             [(picture_vectors, hbm), (caption_vectors, hbm)],
             [fast((taken, width))],
-            [pltpu.VMEM(block, F32), pltpu.SemaphoreType.DMA((CHUNKS,))],
+            [pltpu.VMEM(block, F32), pltpu.SemaphoreType.DMA((4,))],
             cost=cost,
         )
 
@@ -383,7 +385,7 @@
         {13 + i: i for i in range(4)},
     )
     whole = (jax.ShapeDtypeStruct(block, F32), hbm)
-    out_scratch = [pltpu.VMEM(block, F32), pltpu.SemaphoreType.DMA((CHUNKS,))]
+    out_scratch = [pltpu.VMEM(block, F32), pltpu.SemaphoreType.DMA((4,))]
     image_out, text_out, loss_q, loss_p = call(
         second_kernel,
         scalars + v(qh, qlo, y2s, grad_q, loss_q, loss_p, q, inv_q),

time: 59.3 us -> 59.2 us (level)
  no operation moved by 1% of the time
where the time goes in v7:
time: 59.2 us; the launch traced here: 58.9 us
  starting transfers between devices  33 us (56%)
  Pallas kernels  18.5 us (31%)
  waiting for transfers between devices  5.08 us (9%)
  between operations  2.21 us (4%)
    ppermute x3, starting transfers between devices, in_chip(): return lax.ppermute(value, 'blk', [(i, i ^ 1) for i in range(count)])  24.6 us
    pallas_call x9, Pallas kernels, call(): pl.pallas_call(kernel, out_shape=[o for o, _ in outs], in_specs=specs, ou...  18.5 us
    ppermute x3, starting transfers between devices, across(): return lax.ppermute(value, 'blk', pairs)  8.34 us
    ppermute x3, waiting for transfers between devices, in_chip(): return lax.ppermute(value, 'blk', [(i, i ^ 1) for i in range(count)])  4.13 us
  transfers between devices with their start and end apart: 6, of which 4 were waited for; matrix products, arithmetic and copies ran while one was open for 0% of the time, Pallas kernels for 27%

profile of v7, /device:TPU:1, one launch (start us, length us, event | category | flops | bytes accessed | tf_op | source)
XLA Modules:
  0.0 58.9 jit_solution(3262219252446762551)
XLA Ops:
  0.6 1.5 %shard_map.67.p = f32[256,1152]{1,0:T(8,128)S(1)} custom-call(f32[256,1152]{1,0:T(8,128)} %image.5, f32[256,1152]{1,0:T(8,128)} %text.5), custom_call_target="tpu_custom_call" | custom-call | tf_op jit(solution)/shard_map/pallas_call | solution.py:304
  2.1 4.5 %collective-permute-start.3 = (f32[256,1152]{1,0:T(8,128)S(1)}, f32[256,1152]{1,0:T(8,128)}, u32[]{:S(2)}, u32[]{:S(2)}) collective-permute-start(f32[256,1152]{1,0:T(8,128)S(1)} %shard_map.67.p), channel_id=1, source_target_pairs={{0,511},{1,2},{2,1},{3,4},{4,3},{5,6},{6,5},{7,8},{8,7},{9,10},{10... | collective-permute-start | bytes 3538952 | tf_op jit(solution)/shard_map/ppermute | solution.py:26
  6.6 1.5 %shard_map.68.q = f32[264,1152]{1,0:T(8,128)S(1)} custom-call(f32[256,1152]{1,0:T(8,128)} %image.5, f32[256,1152]{1,0:T(8,128)} %text.5), custom_call_target="tpu_custom_call" | custom-call | bytes 8000000 | tf_op jit(solution)/shard_map/pallas_call | solution.py:304
  8.1 17.0 %conditional.1 = (f32[264,1152]{1,0:T(8,128)}) conditional(s32[]{:T(128)} %convert_element_type.3, f32[264,1152]{1,0:T(8,128)S(1)} %shard_map.68.q, f32[264,1152]{1,0:T(8,128)S(1)} %shard_map.68.q), branch_computations={%region_0.0_spmd, %region_1.0_spmd} | conditional | bytes 9732184 | solution.py:343
  8.1 14.4 %collective-permute-start = (f32[264,1152]{1,0:T(8,128)S(1)}, f32[264,1152]{1,0:T(8,128)}, u32[]{:S(2)}, u32[]{:S(2)}) collective-permute-start(f32[264,1152]{1,0:T(8,128)S(1)} %param.1), channel_id=1, source_target_pairs={{0,1},{1,0},{2,3},{3,2},{4,5},{5,4},{6,7},{7,6},{8,9},{9,8},{10,11... | collective-permute-start | bytes 3649544 | tf_op jit(solution)/shard_map/cond/branch_1_fun/ppermute | solution.py:31
  22.5 2.6 %collective-permute-done = f32[264,1152]{1,0:T(8,128)} collective-permute-done((f32[264,1152]{1,0:T(8,128)S(1)}, f32[264,1152]{1,0:T(8,128)}, u32[]{:S(2)}, u32[]{:S(2)}) %collective-permute-start) | collective-permute-done | bytes 1216544 | tf_op jit(solution)/shard_map/cond/branch_1_fun/ppermute | solution.py:31
  25.1 1.9 %collective-permute-start.5 = (f32[264,1152]{1,0:T(8,128)}, f32[264,1152]{1,0:T(8,128)S(1)}, u32[]{:S(2)}, u32[]{:S(2)}) collective-permute-start(f32[264,1152]{1,0:T(8,128)} %get-tuple-element.78.z), channel_id=1, source_target_pairs={{0,511},{1,2},{2,1},{3,4},{4,3},{5,6},{6,5},{7,8},{8,7},{9,10},{10... | collective-permute-start | bytes 3649544 | tf_op jit(solution)/shard_map/ppermute | solution.py:26
  28.3 2.1 %shard_map.69 = (f32[256,1152]{1,0:T(8,128)S(1)}, f32[256,1152]{1,0:T(8,128)S(1)}, f32[256,256]{1,0:T(8,128)S(1)}, f32[256,256]{1,0:T(8,128)S(1)}, bf16[256,1152...) custom-call(f32[1]{0:T(128)S(6)} %copy.29.scale, ...), custom_call_target="tpu_custom_call" | custom-call | bytes 8000000 | tf_op jit(solution)/shard_map/pallas_call | solution.py:304
  30.5 0.0 collective-permute-done.3.value
  30.5 4.5 %collective-permute-start.4 = (f32[256,1152]{1,0:T(8,128)}, f32[256,1152]{1,0:T(8,128)S(1)}, u32[]{:S(2)}, u32[]{:S(2)}) collective-permute-start(f32[256,1152]{1,0:T(8,128)} %collective-permute-done.3.value), channel_id=1, source_target_pairs={{0,1},{1,0},{2,3},{3,2},{4,5},{5,4},{6,7},{7,6},{8,9},{9,8},{10,11... | collective-permute-start | bytes 3538952 | tf_op jit(solution)/shard_map/ppermute | solution.py:31
  35.0 1.4 %shard_map.70 = (bf16[256,1152]{1,0:T(8,128)(2,1)S(1)}, bf16[256,1152]{1,0:T(8,128)(2,1)S(1)}) custom-call(f32[256,1152]{1,0:T(8,128)} %collective-permute-done.3.value), custom_call_target="tpu_custom_call" | custom-call | bytes 4000000 | tf_op jit(solution)/shard_map/pallas_call | solution.py:304
  36.4 1.2 %collective-permute-done.4.y1s = f32[256,1152]{1,0:T(8,128)S(1)} collective-permute-done((f32[256,1152]{1,0:T(8,128)}, f32[256,1152]{1,0:T(8,128)S(1)}, u32[]{:S(2)}, u32[]{:S(2)}) %collective-permute-start.4) | collective-permute-done | bytes 1179680 | tf_op jit(solution)/shard_map/ppermute | solution.py:31
  37.6 1.5 %shard_map.71.after = f32[264,1152]{1,0:T(8,128)S(1)} custom-call(f32[1]{0:T(128)S(6)} %copy.29.scale, f32[1]{0:T(128)S(6)} %copy.30.shift, bf16[256,1152]{1,0:T(8,128)(2,1)S(1)} %get-tuple-element.48.yh, bf16[256,1152]{1,0:T(8,128)(2,1)S(1)} %get-tuple-element.49.yl, f32[256,1152]{1,0:T(8,128)S(1)} %collective-permute-done.4.y1s), custom_call_target="tpu_custom_call" | custom-call | tf_op jit(solution)/shard_map/pallas_call | solution.py:304
  39.1 1.9 %collective-permute-start.6 = (f32[264,1152]{1,0:T(8,128)S(1)}, f32[264,1152]{1,0:T(8,128)S(1)}, u32[]{:S(2)}, u32[]{:S(2)}) collective-permute-start(f32[264,1152]{1,0:T(8,128)S(1)} %shard_map.71.after), channel_id=1, source_target_pairs={{0,511},{1,2},{2,1},{3,4},{4,3},{5,6},{6,5},{7,8},{8,7},{9,10},{10... | collective-permute-start | bytes 3649544 | tf_op jit(solution)/shard_map/ppermute | solution.py:26
  41.1 4.1 %shard_map.72 = (f32[256,1152]{1,0:T(8,128)S(1)}, f32[256,1152]{1,0:T(8,128)S(1)}, f32[256,256]{1,0:T(8,128)S(1)}, f32[256,256]{1,0:T(8,128)S(1)}) custom-call(f32[1]{0:T(128)S(6)} %copy.29.scale, f32[1]{0:T(128)S(6)} %copy.30.shift, ...), custom_call_target="tpu_custom_call", output_to_operand_aliasing={{0}: (10, {}), {1}: (11, {}), {2}: (12, {}), {3}: (13, {})} | custom-call | tf_op jit(solution)/shard_map/pallas_call | solution.py:304
  45.2 0.0 collective-permute-done.5.y2
  45.2 0.1 slice.9
  45.3 5.7 %collective-permute-start.7 = (f32[256,1152]{1,0:T(8,128)S(1)}, f32[256,1152]{1,0:T(8,128)S(1)}, u32[]{:S(2)}, u32[]{:S(2)}) collective-permute-start(f32[256,1152]{1,0:T(8,128)S(1)} %slice.9), channel_id=1, source_target_pairs={{0,1},{1,0},{2,3},{3,2},{4,5},{5,4},{6,7},{7,6},{8,9},{9,8},{10,11... | collective-permute-start | bytes 3538952 | tf_op jit(solution)/shard_map/ppermute | solution.py:31
  51.0 2.2 %shard_map.73 = (f32[256,1152]{1,0:T(8,128)S(1)}, f32[256,1152]{1,0:T(8,128)S(1)}, f32[256,256]{1,0:T(8,128)S(1)}, f32[256,256]{1,0:T(8,128)S(1)}, f32[256,128]{1,0:T(8,128)S(1)}, /*index=5*/f32[256,128]{1,0:T(8,128)S(1)}) custom-call(f32[1]{0:T(128)S(6)} %copy.29.scale, ...), custom_call_target="tpu_custom_call", output_to_operand_aliasing={{0}: (13, {}), {1}: (14, {}), {2}: (15, {}), {3}: (16, {})} | custom-call | tf_op jit(solution)/shard_map/pallas_call | solution.py:304
  53.2 0.3 collective-permute-done.7.y2s
  53.5 2.9 %shard_map.74 = (f32[256,1152]{1,0:T(8,128)}, f32[256,1152]{1,0:T(8,128)}, f32[8,256]{1,0:T(8,128)S(1)}, f32[8,256]{1,0:T(8,128)S(1)}) custom-call(f32[1]{0:T(128)S(6)} %copy.29.scale, f32[1]{0:T(128)S(6)} %copy.30.shift, bf16[256,1152]{1,0:T(8,128)(2,1)S(1)} %get-tuple-element.44.qh, bf16[256,1152]{1,0:T(8,128)(2,1)S(1)} %get-tuple-element.45.qlo, ...), custom_call_target="tpu_custom_call" | custom-call | tf_op jit(solution)/shard_map/pallas_call | solution.py:304
  56.4 0.9 %collective-permute-done.6.returned = f32[264,1152]{1,0:T(8,128)S(1)} collective-permute-done((f32[264,1152]{1,0:T(8,128)S(1)}, f32[264,1152]{1,0:T(8,128)S(1)}, u32[]{:S(2)}, u32[]{:S(2)}) %collective-permute-start.6) | collective-permute-done | bytes 1216544 | tf_op jit(solution)/shard_map/ppermute | solution.py:26
  57.3 1.4 %shard_map.75 = (f32[1,256]{1,0:T(1,128)}, f32[256,1152]{1,0:T(8,128)}, f32[256,1152]{1,0:T(8,128)}) custom-call(f32[256,1152]{1,0:T(8,128)S(1)} %get-tuple-element.63.gp_in, f32[264,1152]{1,0:T(8,128)S(1)} %collective-permute-done.6.returned, f32[256,1152]{1,0:T(8,128)S(1)} %shard_map.67.p, ...), custom_call_target="tpu_custom_call", output_to_operand_aliasing={{1}: (6, {}), {2}: (7, {})} | custom-call | tf_op jit(solution)/shard_map/pallas_call | solution.py:304
Async XLA Ops:
  2.1 28.4 %collective-permute-start.3 = (f32[256,1152]{1,0:T(8,128)S(1)}, f32[256,1152]{1,0:T(8,128)}, u32[]{:S(2)}, u32[]{:S(2)}) collective-permute-start(f32[256,1152]{1,0:T(8,128)S(1)} %shard_map.67.p), channel_id=1, source_target_pairs={{0,511},{1,2},{2,1},{3,4},{4,3},{5,6},{6,5},{7,8},{8,7},{9,10},{10... | collective-permute-start | bytes 3538952 | tf_op jit(solution)/shard_map/ppermute | solution.py:26
  8.1 17.0 %collective-permute-start = (f32[264,1152]{1,0:T(8,128)S(1)}, f32[264,1152]{1,0:T(8,128)}, u32[]{:S(2)}, u32[]{:S(2)}) collective-permute-start(f32[264,1152]{1,0:T(8,128)S(1)} %param.1), channel_id=1, source_target_pairs={{0,1},{1,0},{2,3},{3,2},{4,5},{5,4},{6,7},{7,6},{8,9},{9,8},{10,11... | collective-permute-start | bytes 3649544 | tf_op jit(solution)/shard_map/cond/branch_1_fun/ppermute | solution.py:31
  25.1 20.1 %collective-permute-start.5 = (f32[264,1152]{1,0:T(8,128)}, f32[264,1152]{1,0:T(8,128)S(1)}, u32[]{:S(2)}, u32[]{:S(2)}) collective-permute-start(f32[264,1152]{1,0:T(8,128)} %get-tuple-element.78.z), channel_id=1, source_target_pairs={{0,511},{1,2},{2,1},{3,4},{4,3},{5,6},{6,5},{7,8},{8,7},{9,10},{10... | collective-permute-start | bytes 3649544 | tf_op jit(solution)/shard_map/ppermute | solution.py:26
  30.5 7.2 %collective-permute-start.4 = (f32[256,1152]{1,0:T(8,128)}, f32[256,1152]{1,0:T(8,128)S(1)}, u32[]{:S(2)}, u32[]{:S(2)}) collective-permute-start(f32[256,1152]{1,0:T(8,128)} %collective-permute-done.3.value), channel_id=1, source_target_pairs={{0,1},{1,0},{2,3},{3,2},{4,5},{5,4},{6,7},{7,6},{8,9},{9,8},{10,11... | collective-permute-start | bytes 3538952 | tf_op jit(solution)/shard_map/ppermute | solution.py:31
  39.1 18.2 %collective-permute-start.6 = (f32[264,1152]{1,0:T(8,128)S(1)}, f32[264,1152]{1,0:T(8,128)S(1)}, u32[]{:S(2)}, u32[]{:S(2)}) collective-permute-start(f32[264,1152]{1,0:T(8,128)S(1)} %shard_map.71.after), channel_id=1, source_target_pairs={{0,511},{1,2},{2,1},{3,4},{4,3},{5,6},{6,5},{7,8},{8,7},{9,10},{10... | collective-permute-start | bytes 3649544 | tf_op jit(solution)/shard_map/ppermute | solution.py:26
  45.3 8.2 %collective-permute-start.7 = (f32[256,1152]{1,0:T(8,128)S(1)}, f32[256,1152]{1,0:T(8,128)S(1)}, u32[]{:S(2)}, u32[]{:S(2)}) collective-permute-start(f32[256,1152]{1,0:T(8,128)S(1)} %slice.9), channel_id=1, source_target_pairs={{0,1},{1,0},{2,3},{3,2},{4,5},{5,4},{6,7},{7,6},{8,9},{9,8},{10,11... | collective-permute-start | bytes 3538952 | tf_op jit(solution)/shard_map/ppermute | solution.py:31
